TPU v7x, 32 devices: a whole 2x2x4 slice. The times are simulated.
32 devices in a mesh: groups: 2 (over y), cluster: 4 (over z), helper: 2 (over x), rep: 2 (over core).
Axes of the slice: x: 2, y: 2, z: 4, core: 2. Of those that a mesh axis runs over, the one named last changes fastest.
Arguments:
- embeddings: bfloat16 [8192, 1024], P(('groups', 'cluster', 'helper', 'rep')), parts along dimension 0, may hold values from -6 to 6
- labels: int32 [8192, 1], P(('groups', 'cluster', 'helper', 'rep')), parts along dimension 0, may hold values from 0 to 3; in each aligned block of 256 rows (0 to 255, 256 to 511, ...) at most 128 rows name the same one
- priority: int32 [8192], P(('groups', 'cluster', 'helper', 'rep')), parts along dimension 0, may hold values from 0 to 4095
Outputs:
- best_cosine: float32 [8192], P(('groups', 'cluster', 'helper', 'rep')), parts along dimension 0
There are 2 independent parts, one for each index of `groups`. A program takes and returns all parts, laid end to end along the dimension named above; each array names one. Nothing has to cross between parts.
Inputs may be any that keep to these rules, and one draw needn't show every extreme that they name: `labels`: in the rows of one device no cluster is named more than 128 times, and in some devices' rows some cluster exactly 128 times; every cluster is named.
All inputs are finite; a program needn't handle non-finite values.
Results may differ from a plain program's by a relative error of at most 0.0014.
Values may be sent and summed in bfloat16 or wider, within the bound.
No kernel may reach another device: no remote copies, remote signals or barrier semaphores. Data moves between devices by JAX's collectives and lax.ppermute only.
A program may use at most 64 MiB of HBM per device.

v0:
```python
import jax
import jax.numpy as jnp
from jax import lax
from jax.sharding import PartitionSpec as P

sentinel_key = 2147483647


def pair_scores(queries, key_rows):
    return lax.dot_general(
        queries, key_rows, (((1,), (1,)), ((), ())), preferred_element_type=jnp.float32
    )


def body(embeddings, labels, priority):
    rows_here = embeddings.shape[0]
    width = embeddings.shape[1]
    owners = lax.axis_size("cluster")
    slot_count = 2 * rows_here
    capacity = slot_count // owners
    row_total = rows_here * lax.axis_size(("cluster", "helper", "rep"))
    widened = embeddings.astype(jnp.float32)
    unit_rows = (
        widened * lax.rsqrt(jnp.sum(widened * widened, axis=1, keepdims=True) + 1e-06)
    ).astype(jnp.bfloat16)
    local_index = jnp.arange(rows_here, dtype=jnp.int32)
    order_key = (
        priority * row_total
        + lax.axis_index(("cluster", "helper", "rep")) * rows_here
        + local_index
    )
    row_label = labels[:, 0]
    same_cluster = row_label[:, None] == row_label[None, :]
    before = local_index[:, None] > local_index[None, :]
    local_rank = jnp.sum(same_cluster & before, axis=1)
    slot_index = row_label * capacity + local_rank
    send_unit = jnp.zeros((slot_count, width), jnp.bfloat16).at[slot_index].set(unit_rows)
    send_key = jnp.full((slot_count,), sentinel_key, jnp.int32).at[slot_index].set(order_key)
    recv_unit, recv_key = (
        lax.all_to_all(
            send_unit.reshape(owners, capacity, width),
            "cluster",
            split_axis=0,
            concat_axis=0,
            tiled=True,
        ),
        lax.all_to_all(
            send_key.reshape(owners, capacity), "cluster", split_axis=0, concat_axis=0, tiled=True
        ),
    )
    queries = recv_unit.reshape(slot_count, width)
    query_key = recv_key.reshape(slot_count)
    start_best = jnp.full((slot_count,), -1.0, jnp.float32)
    key_rows = lax.all_gather(queries, ("helper", "rep"), axis=0, tiled=True)
    key_order = lax.all_gather(query_key, ("helper", "rep"), axis=0, tiled=True)
    scores = pair_scores(queries, key_rows)
    earlier = key_order[None, :] < query_key[:, None]
    best_score = jnp.maximum(start_best, jnp.max(jnp.where(earlier, scores, -1.0), axis=1))
    back_home = lax.all_to_all(
        best_score.reshape(owners, capacity), "cluster", split_axis=0, concat_axis=0, tiled=True
    )
    return back_home.reshape(slot_count)[slot_index]


def solution(mesh):
    in_specs = (
        P(("groups", "cluster", "helper", "rep"), None),
        P(("groups", "cluster", "helper", "rep"), None),
        P(("groups", "cluster", "helper", "rep")),
    )
    out_specs = P(("groups", "cluster", "helper", "rep"))
    return jax.shard_map(body, mesh=mesh, in_specs=in_specs, out_specs=out_specs, check_vma=False)
```

profile of v0, /device:TPU:0, one launch (start us, length us, event | category | flops | bytes accessed | tf_op | source)
XLA Modules:
  0.0 102.6 jit_solution(8283583324609745790)
XLA Ops:
  6.5 0.0 copy-start
  6.5 0.0 all-gather.3.cloned.1.call-start
  6.5 0.9 convert_reduce_fusion
  7.5 0.7 compare_select_fusion
  8.2 1.2 %fusion = f32[256]{0:T(256)S(1)} fusion(bf16[256,1024]{1,0:T(8,128)(2,1)} %param.3), kind=kLoop, calls=%fused_computation.6 | loop fusion | flops 786176 | bytes 525312 | tf_op jit(solution)/shard_map/reduce_sum | solution.py:24
  9.4 2.5 %scatter_custom_fusion.1 = bf16[512,1024]{1,0:T(8,128)(2,1)S(1)} fusion(s32[256]{0:T(256)S(1)} %bitcast.22, bf16[256,1024]{1,0:T(8,128)(2,1)} %param.3, f32[256]{0:T(256)S(1)} %add_rsqrt_fusion, bf16[]{:T(256)} %constant.14.clone.1), kind=kCustom, calls=%fused_computation.8 | custom fusion | flops 786432 | bytes 1573890 | tf_op jit(solution)/shard_map/scatter | solution.py:37
  11.9 31.9 %all_to_all.20 = bf16[4,128,1024]{2,1,0:T(8,128)(2,1)} all-to-all(bf16[4,128,1024]{2,1,0:T(8,128)(2,1)S(1)} %bitcast.16), channel_id=1, replica_groups=mesh['groups'=2,'cluster'=4,'helper'=2,'rep'=2] {'cluster'}, dimensions={0} | all-to-all | bytes 2097152 | tf_op jit(solution)/shard_map/all_to_all | solution.py:40
  43.8 0.0 all-gather.3.cloned.1.call-update
  43.9 0.0 copy-done
  43.9 1.4 %scatter_custom_fusion = s32[512]{0:T(512)S(1)} fusion(s32[256]{0:T(256)S(1)} %bitcast.23, s32[256]{0:T(256)S(1)} %iota_add_fusion, s32[]{:T(128)} %constant.16.clone.1), kind=kCustom, calls=%fused_computation.19 | custom fusion | bytes 2052 | tf_op jit(solution)/shard_map/scatter | solution.py:38
  45.3 8.1 %all_to_all.21 = s32[4,1,128]{2,1,0:T(1,128)S(1)} all-to-all(s32[4,1,128]{2,1,0:T(1,128)S(1)} %bitcast.21), channel_id=1, replica_groups=mesh['groups'=2,'cluster'=4,'helper'=2,'rep'=2] {'cluster'}, dimensions={0} | all-to-all | bytes 4096 | tf_op jit(solution)/shard_map/all_to_all | solution.py:47
  53.4 5.2 %all-gather = s32[4,1,512]{2,1,0:T(1,128)S(1)} all-gather(s32[1,1,512]{2,1,0:T(1,128)S(1)} %bitcast.19), channel_id=1, replica_groups=mesh['groups'=2,'cluster'=4,'helper'=2,'rep'=2] {'helper','rep'}, dimensions={0}, use_global_device_ids=true | all-gather | bytes 10240 | tf_op jit(solution)/shard_map/all_gather | solution.py:55
  58.5 19.1 %all-gather.3.cloned.1.call-done = bf16[2048,1024]{1,0:T(8,128)(2,1)} async-done(((bf16[512,1024]{1,0:T(8,128)(2,1)}), bf16[2048,1024]{1,0:T(8,128)(2,1)}) %all-gather.3.cloned.1.call-update) | async-done | bytes 4194320 | tf_op jit(solution)/shard_map/all_gather | solution.py:54
  77.6 5.0 %select_reduce_fusion = f32[512]{0:T(512)S(1)} fusion(bf16[512,1024]{1,0:T(8,128)(2,1)} %bitcast.15, bf16[2048,1024]{1,0:T(8,128)(2,1)} %all-gather.3.cloned.1.call-done, s32[2048]{0:T(1024)S(1)} %bitcast.18, s32[512]{0:T(512)S(1)} %bitcast.20), kind=kOutput, calls=%fused_computation.3 | convolution fusion | flops 2150628864 | bytes 5255168 | tf_op jit(solution)/shard_map/dot_general | solution.py:10
  82.6 0.6 broadcast_maximum_fusion
  83.2 4.6 %all-to-all-start.2 = ((f32[4,1,128]{2,1,0:T(1,128)}), f32[4,1,128]{2,1,0:T(1,128)S(1)}, u32[]{:S(2)}, u32[]{:S(2)}) async-start(f32[4,1,128]{2,1,0:T(1,128)} %bitcast.9), calls=%async_computation.2 | async-start | bytes 4096 | tf_op jit(solution)/shard_map/all_to_all | solution.py:59
  87.8 5.4 %all-to-all-done.2 = f32[4,1,128]{2,1,0:T(1,128)S(1)} async-done(((f32[4,1,128]{2,1,0:T(1,128)}), f32[4,1,128]{2,1,0:T(1,128)S(1)}, u32[]{:S(2)}, u32[]{:S(2)}) %all-to-all-start.2) | async-done | bytes 2080 | tf_op jit(solution)/shard_map/all_to_all | solution.py:59
  93.2 2.5 %gather_fusion = f32[256]{0:T(256)} fusion(f32[512]{0:T(512)S(1)} %bitcast.13, s32[1024]{0:T(1024)S(1)} %pad_clamp_fusion), kind=kCustom, calls=%fused_computation | custom fusion | bytes 3072 | tf_op jit(solution)/shard_map/gather | solution.py:62
  (3 shorter events, 0.0 us)
Async XLA Ops:
  6.5 37.3 %copy-start = (s32[256]{0:T(256)S(1)}, s32[256]{0:T(256)}, u32[]{:S(2)}) copy-start(s32[256]{0:T(256)} %param.5) | copy-start | bytes 3076
  6.5 71.1 %all-gather.3.cloned.1.call-start = ((), (), s32[]{:S(2)}) async-start(), calls=%async_computation.3 | async-start | bytes 5242880 | tf_op jit(solution)/shard_map/all_gather | solution.py:54
  83.2 10.0 %all-to-all-start.2 = ((f32[4,1,128]{2,1,0:T(1,128)}), f32[4,1,128]{2,1,0:T(1,128)S(1)}, u32[]{:S(2)}, u32[]{:S(2)}) async-start(f32[4,1,128]{2,1,0:T(1,128)} %bitcast.9), calls=%async_computation.2 | async-start | bytes 4096 | tf_op jit(solution)/shard_map/all_to_all | solution.py:59
Sparse Core Ops, SparseCore 0:
  44.0 33.6 all-gather.2
where the time goes:
time: 103 us
  blocking collectives  45.2 us (44%)
  waiting for transfers between devices  24.5 us (24%)
  between operations  13.4 us (13%)
  other arithmetic  5.95 us (6%)
  matrix products  4.98 us (5%)
  starting transfers between devices  4.6 us (4%)
  local copies, waits for them, and re-layouts  3.9 us (4%)
    all_to_all x1, blocking collectives, body(): lax.all_to_all(send_unit.reshape(owners, capacity, width), 'cluster', spl...  31.9 us
    all_gather x1, waiting for transfers between devices, body(): key_rows = lax.all_gather(queries, ('helper', 'rep'), axis=0, tiled=True)  19.1 us
    all_to_all x1, blocking collectives, body(): lax.all_to_all(send_key.reshape(owners, capacity), 'cluster', split_axis=...  8.08 us
    all_to_all x1, waiting for transfers between devices, body(): lax.all_to_all(best_score.reshape(owners, capacity), 'cluster', split_axi...  5.38 us
    all_gather x1, blocking collectives, body(): key_order = lax.all_gather(query_key, ('helper', 'rep'), axis=0, tiled=True)  5.16 us
    dot_general x1, matrix products, pair_scores(): lax.dot_general(queries, key_rows, (((1,), (1,)), ((), ())), preferred_el...  4.98 us
    all_to_all x1, starting transfers between devices, body(): lax.all_to_all(best_score.reshape(owners, capacity), 'cluster', split_axi...  4.6 us
    gather x1, local copies, waits for them, and re-layouts, body(): return back_home.reshape(slot_count)[slot_index]  2.5 us
  transfers between devices with their start and end apart: 2, of which 2 were waited for; matrix products, arithmetic and copies ran while one was open for 1% of the time, Pallas kernels for 0%

commit v1 on v0

v1 whole, which is shorter than its diff:
```python
import jax
import jax.numpy as jnp
from jax import lax
from jax.experimental import pallas as pl
from jax.experimental.pallas import tpu as pltpu
from jax.sharding import PartitionSpec as P

VMEM_BYTES = 40 * 1024 * 1024


def unit(raw):
    wide = raw.astype(jnp.float32)
    scale = lax.rsqrt(jnp.sum(wide * wide, axis=1, keepdims=True) + 1e-06)
    return (wide * scale).astype(jnp.bfloat16)


def as_column(row):
    parts = [
        jnp.broadcast_to(row[:, i : i + 128], (128, 128)).T for i in range(0, row.shape[1], 128)
    ]
    return jnp.concatenate(parts, axis=0)


def score_block(left, right, left_label, left_key, right_meta):
    scores = lax.dot_general(
        left, right, (((1,), (1,)), ((), ())), preferred_element_type=jnp.float32
    )
    for_left, for_right = None, []
    for i in range(0, scores.shape[1], 128):
        tile = scores[:, i : i + 128]
        label, key = right_meta[0:1, i : i + 128], right_meta[1:2, i : i + 128]
        tile = jnp.where(left_label == label, tile, -1.0)
        earlier = key < left_key
        mine = jnp.where(earlier, tile, -1.0)
        for_left = mine if for_left is None else jnp.maximum(for_left, mine)
        theirs = jnp.where(left_key < key, tile, -1.0)
        for_right.append(jnp.max(theirs, axis=0, keepdims=True))
    return for_left, jnp.concatenate(for_right, axis=1)


def as_row(column_best):
    parts = [
        jnp.max(column_best[i : i + 128, :].T, axis=0, keepdims=True)
        for i in range(0, column_best.shape[0], 128)
    ]
    return jnp.concatenate(parts, axis=1)


def plane_kernel(count, *refs):
    blocks, metas = refs[:count], refs[count : 2 * count]
    unit_out, own_out = refs[2 * count :]
    rows = blocks[0].shape[0]
    own = unit(blocks[0][...])
    own_label, own_key = as_column(metas[0][0:1, :]), as_column(metas[0][1:2, :])
    best = None
    for i in range(count):
        right = own if i == 0 else unit(blocks[i][...])
        unit_out[i * rows : (i + 1) * rows, :] = right
        here, _ = score_block(own, right, own_label, own_key, metas[i][...])
        best = here if best is None else jnp.maximum(best, here)
    own_out[...] = as_row(best)


def pair_kernel(count, reps, has_sum, *refs):
    unit_ref, other_ref, other_meta = refs[:3]
    metas = refs[3 : 3 + count]
    refs = refs[3 + count :]
    sums = refs[:reps] if has_sum else None
    outs = refs[reps:] if has_sum else refs
    other_out = outs[reps]
    rows = other_ref.shape[0]
    other = unit(other_ref[...])
    label, key = as_column(other_meta[0:1, :]), as_column(other_meta[1:2, :])
    best = None
    for i in range(count):
        right = unit_ref[i * rows : (i + 1) * rows, :]
        here, there = score_block(other, right, label, key, metas[i][...])
        best = here if best is None else jnp.maximum(best, here)
        shift, rep = i // reps, i % reps
        if has_sum:
            there = jnp.maximum(there, sums[rep][shift : shift + 1, :])
        outs[rep][shift : shift + 1, :] = there
    other_out[...] = as_row(best)


def kernel_call(kernel, out_shape, operands, flops):
    whole = pl.BlockSpec(memory_space=pltpu.VMEM)
    return pl.pallas_call(
        kernel,
        out_shape=out_shape,
        in_specs=[whole] * len(operands),
        out_specs=[whole] * len(out_shape),
        compiler_params=pltpu.CompilerParams(vmem_limit_bytes=VMEM_BYTES),
        cost_estimate=pl.CostEstimate(
            flops=flops,
            bytes_accessed=sum(o.size * o.dtype.itemsize for o in operands),
            transcendentals=0,
        ),
    )(*operands)


def body(embeddings, labels, priority):
    rows, width = embeddings.shape
    owners, helpers, reps = (lax.axis_size(a) for a in ("cluster", "helper", "rep"))
    row_total = rows * owners * helpers * reps
    count = helpers * reps
    place = lax.axis_index(("cluster", "helper", "rep"))
    order_key = priority * row_total + place * rows + jnp.arange(rows, dtype=jnp.int32)
    meta = jnp.stack([labels[:, 0] + 1, order_key])

    def shifted(value, axis, size, shift):
        return lax.ppermute(value, axis, [((i + shift) % size, i) for i in range(size)])

    steps = [[(i, (i + d) % owners) for i in range(owners)] for d in range(1, (owners + 1) // 2)]
    backs = [[(b, a) for a, b in step] for step in steps]
    if owners % 2 == 0:
        half = owners // 2
        steps.append([(i, i + half) if i % 2 == 0 else (i + half, i) for i in range(half)])
        backs.append([(i, (i + half) % owners) for i in range(owners)])
    others = [lax.ppermute(embeddings, "cluster", step) for step in steps]

    def plane(value):
        result = []
        for h in range(helpers):
            base = value if h == 0 else shifted(value, "helper", helpers, h)
            for r in range(reps):
                result.append(base if r == 0 else shifted(base, "rep", reps, r))
        return result

    blocks = plane(embeddings)
    metas = plane(meta)
    other_metas = [lax.ppermute(meta, "cluster", step) for step in steps]

    f32 = jnp.float32
    units, own_best = kernel_call(
        lambda *refs: plane_kernel(count, *refs),
        [
            jax.ShapeDtypeStruct((count * rows, width), jnp.bfloat16),
            jax.ShapeDtypeStruct((1, rows), f32),
        ],
        blocks + metas,
        2 * count * rows * rows * width,
    )
    sums, returned = [], []
    for other, other_meta, back in zip(others, other_metas, backs):
        has_sum = bool(sums)
        *sums, other_best = kernel_call(
            lambda *refs, has_sum=has_sum: pair_kernel(count, reps, has_sum, *refs),
            [jax.ShapeDtypeStruct((helpers, rows), f32)] * reps
            + [jax.ShapeDtypeStruct((1, rows), f32)],
            [units, other, other_meta] + metas + list(sums),
            2 * count * rows * rows * width,
        )
        returned.append(lax.ppermute(other_best, "cluster", back))
    total = sums[0]
    for r in range(1, reps):
        total = jnp.maximum(total, shifted(sums[r], "rep", reps, reps - r))
    best = jnp.maximum(own_best, total[0:1])
    for h in range(1, helpers):
        best = jnp.maximum(best, shifted(total[h : h + 1], "helper", helpers, helpers - h))
    for value in returned:
        best = jnp.maximum(best, value)
    return best[0]


def solution(mesh):
    axes = ("groups", "cluster", "helper", "rep")
    in_specs = (P(axes, None), P(axes, None), P(axes))
    return jax.shard_map(body, mesh=mesh, in_specs=in_specs, out_specs=P(axes), check_vma=False)
```

time: 103 us -> 40.2 us (0.39)
  blocking collectives: 45.2 us -> 0 us
  starting transfers between devices: 4.6 us -> 21.3 us
  between operations: 13.4 us -> 0.11 us
  waiting for transfers between devices: 24.5 us -> 12.1 us
  matrix products: 4.98 us -> 0 us
  other arithmetic: 5.95 us -> 1.95 us
  Pallas kernels: 0 us -> 3.48 us
  local copies, waits for them, and re-layouts: 3.9 us -> 1.04 us
    all_to_all x2 -> x0, blocking collectives: 40 us -> none  [the longest x1 31.9 us: body(): lax.all_to_all(send_unit.reshape(owners, capacity, width), 'cluster', spl...]
    ppermute x0 -> x14, starting transfers between devices: none -> 21.3 us  [the longest x8 6.55 us: shifted(): lax.ppermute(value, axis, [((i + shift) % size, i) for i in range(size)])]
    all_gather x1 -> x0, waiting for transfers between devices: 19.1 us -> none  [body(): key_rows = lax.all_gather(queries, ('helper', 'rep'), axis=0, tiled=True)]
    ppermute x0 -> x14, waiting for transfers between devices: none -> 12.1 us  [the longest x8 11.4 us: shifted(): lax.ppermute(value, axis, [((i + shift) % size, i) for i in range(size)])]
    all_to_all x1 -> x0, waiting for transfers between devices: 5.38 us -> none  [body(): lax.all_to_all(best_score.reshape(owners, capacity), 'cluster', split_axi...]
    all_gather x1 -> x0, blocking collectives: 5.16 us -> none  [body(): key_order = lax.all_gather(query_key, ('helper', 'rep'), axis=0, tiled=True)]
    dot_general x1 -> x0, matrix products: 4.98 us -> none  [pair_scores(): lax.dot_general(queries, key_rows, (((1,), (1,)), ((), ())), preferred_el...]
    all_to_all x1 -> x0, starting transfers between devices: 4.6 us -> none  [body(): lax.all_to_all(best_score.reshape(owners, capacity), 'cluster', split_axi...]
  transfers between devices with their start and end apart: 2 -> 14, of which waited for: 2 -> 7; matrix products, arithmetic and copies ran while one was open for 1% -> 3% of each run, Pallas kernels for 0% -> 6%
where the time goes in v1:
time: 40.2 us; the launch traced here: 40 us
  starting transfers between devices  21.3 us (53%)
  waiting for transfers between devices  12.1 us (30%)
  Pallas kernels  3.48 us (9%)
  other arithmetic  1.95 us (5%)
  local copies, waits for them, and re-layouts  1.04 us (3%)
    ppermute x8, waiting for transfers between devices, shifted(): lax.ppermute(value, axis, [((i + shift) % size, i) for i in range(size)])  11.4 us
    ppermute x8, starting transfers between devices, shifted(): lax.ppermute(value, axis, [((i + shift) % size, i) for i in range(size)])  6.55 us
    ppermute x2, starting transfers between devices, body(): other_metas = [lax.ppermute(meta, 'cluster', step) for step in steps]  6.31 us
    ppermute x2, starting transfers between devices, body(): others = [lax.ppermute(embeddings, 'cluster', step) for step in steps]  6.09 us
    pallas_call x3, Pallas kernels, kernel_call(): pl.pallas_call(kernel, out_shape=out_shape, in_specs=[whole] * len(operan...  3.48 us
    ppermute x2, starting transfers between devices, body(): returned.append(lax.ppermute(other_best, 'cluster', back))  2.37 us
    unnamed x2, local copies, waits for them, and re-layouts  1.04 us
  transfers between devices with their start and end apart: 14, of which 7 were waited for; matrix products, arithmetic and copies ran while one was open for 3% of the time, Pallas kernels for 6%

profile of v1, /device:TPU:0, one launch (start us, length us, event | category | flops | bytes accessed | tf_op | source)
XLA Modules:
  0.0 40.0 jit_solution(7166968355676493118)
XLA Ops:
  0.0 2.9 %collective-permute-start.1 = (bf16[256,1024]{1,0:T(8,128)(2,1)}, bf16[256,1024]{1,0:T(8,128)(2,1)S(1)}, u32[]{:S(2)}, u32[]{:S(2)}) collective-permute-start(bf16[256,1024]{1,0:T(8,128)(2,1)} %refs_0_.1), channel_id=1, source_target_pairs={{2,0},{0,2},{3,1},{1,3},{6,4},{4,6},{7,5},{5,7},{10,8},{8,10},{11,... | collective-permute-start | bytes 1572872 | tf_op jit(solution)/shard_map/ppermute | solution.py:112
  2.9 0.0 collective-permute-start
  2.9 1.6 %collective-permute-start.8 = (bf16[256,1024]{1,0:T(8,128)(2,1)}, bf16[256,1024]{1,0:T(8,128)(2,1)S(1)}, u32[]{:S(2)}, u32[]{:S(2)}) collective-permute-start(bf16[256,1024]{1,0:T(8,128)(2,1)} %refs_0_.1), channel_id=1, source_target_pairs={{0,4},{4,8},{8,12},{12,0},{1,5},{5,9},{9,13},{13,1},{2,6},{6,10},{... | collective-permute-start | bytes 1572872 | tf_op jit(solution)/shard_map/ppermute | solution.py:120
  4.5 4.5 %collective-permute-start.6 = (bf16[256,1024]{1,0:T(8,128)(2,1)}, bf16[256,1024]{1,0:T(8,128)(2,1)S(1)}, u32[]{:S(2)}, u32[]{:S(2)}) collective-permute-start(bf16[256,1024]{1,0:T(8,128)(2,1)} %refs_0_.1), channel_id=1, source_target_pairs={{0,8},{12,4},{1,9},{13,5},{2,10},{14,6},{3,11},{15,7},{16,24},{28,... | collective-permute-start | bytes 1572872 | tf_op jit(solution)/shard_map/ppermute | solution.py:120
  9.0 6.0 %collective-permute-done.1.refs_2_ = bf16[256,1024]{1,0:T(8,128)(2,1)S(1)} collective-permute-done((bf16[256,1024]{1,0:T(8,128)(2,1)}, bf16[256,1024]{1,0:T(8,128)(2,1)S(1)}, u32[]{:S(2)}, u32[]{:S(2)}) %collective-permute-start.1) | collective-permute-done | bytes 524320 | tf_op jit(solution)/shard_map/ppermute | solution.py:112
  15.1 0.0 collective-permute-start.2
  15.1 0.7 %add_bitcast_fusion = s32[1,256]{1,0:T(1,128)S(1)} fusion(s32[256,1]{0,1:T(1,128)} %param.4), kind=kLoop, calls=%fused_computation.5 | loop fusion | flops 256 | bytes 2048 | tf_op jit(solution)/shard_map/add | solution.py:109
  15.8 0.7 %iota_add_fusion = s32[256]{0:T(256)S(1)} fusion(s32[256]{0:T(256)} %param.5, s32[]{:T(128)S(6)} %mul.19), kind=kLoop, calls=%fused_computation.4 | loop fusion | flops 768 | bytes 2052 | tf_op jit(solution)/shard_map/add | solution.py:108
  16.5 1.8 %collective-permute-start.4 = (s32[2,256]{1,0:T(2,128)S(1)}, s32[2,256]{1,0:T(2,128)S(1)}, u32[]{:S(2)}, u32[]{:S(2)}) collective-permute-start(s32[2,256]{1,0:T(2,128)S(1)} %pad_add_fusion.refs_4_.refs_3_), channel_id=1, source_target_pairs={{2,0},{0,2},{3,1},{1,3},{6,4},{4,6},{7,5},{5,7},{10,8},{8,10},{11,... | collective-permute-start | bytes 6152 | tf_op jit(solution)/shard_map/ppermute | solution.py:112
  18.3 1.8 %collective-permute-done.4.refs_6_.refs_5_ = s32[2,256]{1,0:T(2,128)S(1)} collective-permute-done((s32[2,256]{1,0:T(2,128)S(1)}, s32[2,256]{1,0:T(2,128)S(1)}, u32[]{:S(2)}, u32[]{:S(2)}) %collective-permute-start.4) | collective-permute-done | bytes 2080 | tf_op jit(solution)/shard_map/ppermute | solution.py:112
  20.1 0.0 collective-permute-start.3
  20.1 1.2 %collective-permute-done.3.refs_5_.refs_4_ = s32[2,256]{1,0:T(2,128)S(1)} collective-permute-done((s32[2,256]{1,0:T(2,128)S(1)}, s32[2,256]{1,0:T(2,128)S(1)}, u32[]{:S(2)}, u32[]{:S(2)}) %collective-permute-start.3) | collective-permute-done | bytes 2080 | tf_op jit(solution)/shard_map/ppermute | solution.py:112
  21.3 0.2 collective-permute-start.5
  21.4 1.0 %collective-permute-done.5.refs_7_.refs_6_ = s32[2,256]{1,0:T(2,128)S(1)} collective-permute-done((s32[2,256]{1,0:T(2,128)S(1)}, s32[2,256]{1,0:T(2,128)S(1)}, u32[]{:S(2)}, u32[]{:S(2)}) %collective-permute-start.5) | collective-permute-done | bytes 2080 | tf_op jit(solution)/shard_map/ppermute | solution.py:112
  22.4 1.8 %collective-permute-start.9 = (s32[2,256]{1,0:T(2,128)S(1)}, s32[2,256]{1,0:T(2,128)S(1)}, u32[]{:S(2)}, u32[]{:S(2)}) collective-permute-start(s32[2,256]{1,0:T(2,128)S(1)} %pad_add_fusion.refs_4_.refs_3_), channel_id=1, source_target_pairs={{0,4},{4,8},{8,12},{12,0},{1,5},{5,9},{9,13},{13,1},{2,6},{6,10},{... | collective-permute-start | bytes 6152 | tf_op jit(solution)/shard_map/ppermute | solution.py:132
  24.2 0.0 collective-permute-done.refs_1_
  24.2 4.5 %collective-permute-start.7 = (s32[2,256]{1,0:T(2,128)S(1)}, s32[2,256]{1,0:T(2,128)S(1)}, u32[]{:S(2)}, u32[]{:S(2)}) collective-permute-start(s32[2,256]{1,0:T(2,128)S(1)} %pad_add_fusion.refs_4_.refs_3_), channel_id=1, source_target_pairs={{0,8},{12,4},{1,9},{13,5},{2,10},{14,6},{3,11},{15,7},{16,24},{28,... | collective-permute-start | bytes 6152 | tf_op jit(solution)/shard_map/ppermute | solution.py:132
  28.7 0.0 collective-permute-done.2.refs_3_
  28.7 0.0 copy-start
  28.8 1.0 %copy-done = bf16[256,1024]{1,0:T(8,128)(2,1)S(1)} copy-done((bf16[256,1024]{1,0:T(8,128)(2,1)S(1)}, bf16[256,1024]{1,0:T(8,128)(2,1)}, u32[]{:S(2)}) %copy-start) | copy-done | bytes 524312
  29.8 1.3 %shard_map.37 = (bf16[1024,1024]{1,0:T(8,128)(2,1)S(1)}, f32[1,256]{1,0:T(1,128)S(1)}) custom-call(bf16[256,1024]{1,0:T(8,128)(2,1)S(1)} %copy-done, bf16[256,1024]{1,0:T(8,128)(2,1)S(1)} %collective-permute-done.refs_1_, bf16[256,1024]{1,0:T(8,128)(2,1)S(1)} %collective-permute-done.1.refs_2_, bf16[256,1024]{1,0:T(8,128)(2,1)S(1)} %collective-permute-done.2.refs_3_, ...), custom_call_target="tpu_custom_call" | custom-call | flops 536870912 | bytes 2105344 | tf_op jit(solution)/shard_map/pallas_call | solution.py:88
  31.1 0.0 collective-permute-done.9.refs_2_
  31.1 0.0 collective-permute-done.8.refs_1_
  31.1 1.1 %shard_map.38 = (f32[2,256]{1,0:T(2,128)S(1)}, f32[2,256]{1,0:T(2,128)S(1)}, f32[1,256]{1,0:T(1,128)S(1)}) custom-call(bf16[1024,1024]{1,0:T(8,128)(2,1)S(1)} %get-tuple-element.14.refs_0_, bf16[256,1024]{1,0:T(8,128)(2,1)S(1)} %collective-permute-done.8.refs_1_, s32[2,256]{1,0:T(2,128)S(1)} %collective-permute-done.9.refs_2_, ...), custom_call_target="tpu_custom_call" | custom-call | flops 536870912 | bytes 2631680 | tf_op jit(solution)/shard_map/pallas_call | solution.py:88
  32.2 0.0 collective-permute-done.7.refs_2_
  32.2 0.0 collective-permute-done.6.refs_1_
  32.2 1.1 %shard_map.39 = (f32[2,256]{1,0:T(2,128)S(1)}, f32[2,256]{1,0:T(2,128)S(1)}, f32[1,256]{1,0:T(1,128)S(1)}) custom-call(bf16[1024,1024]{1,0:T(8,128)(2,1)S(1)} %get-tuple-element.14.refs_0_, bf16[256,1024]{1,0:T(8,128)(2,1)S(1)} %collective-permute-done.6.refs_1_, s32[2,256]{1,0:T(2,128)S(1)} %collective-permute-done.7.refs_2_, ...), custom_call_target="tpu_custom_call" | custom-call | flops 536870912 | bytes 2635776 | tf_op jit(solution)/shard_map/pallas_call | solution.py:88
  33.3 0.1 collective-permute-start.10
  33.4 1.0 %collective-permute-start.13 = (f32[1,256]{1,0:T(1,128)S(1)}, f32[1,256]{1,0:T(1,128)S(1)}, u32[]{:S(2)}, u32[]{:S(2)}) collective-permute-start(f32[1,256]{1,0:T(1,128)S(1)} %get-tuple-element.20), channel_id=1, source_target_pairs={{0,8},{4,12},{8,0},{12,4},{1,9},{5,13},{9,1},{13,5},{2,10},{6,14},... | collective-permute-start | bytes 3080 | tf_op jit(solution)/shard_map/ppermute | solution.py:154
  34.4 1.3 %collective-permute-start.12 = (f32[1,256]{1,0:T(1,128)S(1)}, f32[1,256]{1,0:T(1,128)S(1)}, u32[]{:S(2)}, u32[]{:S(2)}) collective-permute-start(f32[1,256]{1,0:T(1,128)S(1)} %get-tuple-element.19), channel_id=1, source_target_pairs={{4,0},{8,4},{12,8},{0,12},{5,1},{9,5},{13,9},{1,13},{6,2},{10,6},{... | collective-permute-start | bytes 3080 | tf_op jit(solution)/shard_map/ppermute | solution.py:154
  35.8 0.0 collective-permute-done.10
  35.8 1.6 %collective-permute-start.11 = (f32[1,256]{1,0:T(1,128)S(1)}, f32[1,256]{1,0:T(1,128)S(1)}, u32[]{:S(2)}, u32[]{:S(2)}) collective-permute-start(f32[1,256]{1,0:T(1,128)S(1)} %slice.9), channel_id=1, source_target_pairs={{2,0},{0,2},{3,1},{1,3},{6,4},{4,6},{7,5},{5,7},{10,8},{8,10},{11,... | collective-permute-start | bytes 3080 | tf_op jit(solution)/shard_map/ppermute | solution.py:112
  37.4 0.6 %collective-permute-done.13 = f32[1,256]{1,0:T(1,128)S(1)} collective-permute-done((f32[1,256]{1,0:T(1,128)S(1)}, f32[1,256]{1,0:T(1,128)S(1)}, u32[]{:S(2)}, u32[]{:S(2)}) %collective-permute-start.13) | collective-permute-done | bytes 1056 | tf_op jit(solution)/shard_map/ppermute | solution.py:154
  37.9 0.1 collective-permute-done.12
  38.0 1.4 %collective-permute-done.11 = f32[1,256]{1,0:T(1,128)S(1)} collective-permute-done((f32[1,256]{1,0:T(1,128)S(1)}, f32[1,256]{1,0:T(1,128)S(1)}, u32[]{:S(2)}, u32[]{:S(2)}) %collective-permute-start.11) | collective-permute-done | bytes 1056 | tf_op jit(solution)/shard_map/ppermute | solution.py:112
  39.4 0.6 %fusion.2 = f32[1,256]{1,0:T(1,128)} fusion(f32[1,256]{1,0:T(1,128)S(1)} %collective-permute-done.13, f32[1,256]{1,0:T(1,128)S(1)} %collective-permute-done.12, f32[1,256]{1,0:T(1,128)S(1)} %collective-permute-done.11, f32[1,256]{1,0:T(1,128)S(1)} %get-tuple-element.13, f32[2,256]{1,0:T(2,128)S(1)} %max.15), kind=kLoop, calls=%fused_computation.6 | loop fusion | flops 1024 | bytes 6144 | tf_op jit(solution)/shard_map/max | solution.py:162
  (3 shorter events, 0.0 us)
Async XLA Ops:
  0.0 15.1 %collective-permute-start.1 = (bf16[256,1024]{1,0:T(8,128)(2,1)}, bf16[256,1024]{1,0:T(8,128)(2,1)S(1)}, u32[]{:S(2)}, u32[]{:S(2)}) collective-permute-start(bf16[256,1024]{1,0:T(8,128)(2,1)} %refs_0_.1), channel_id=1, source_target_pairs={{2,0},{0,2},{3,1},{1,3},{6,4},{4,6},{7,5},{5,7},{10,8},{8,10},{11,... | collective-permute-start | bytes 1572872 | tf_op jit(solution)/shard_map/ppermute | solution.py:112
  2.9 21.3 %collective-permute-start = (bf16[256,1024]{1,0:T(8,128)(2,1)}, bf16[256,1024]{1,0:T(8,128)(2,1)S(1)}, u32[]{:S(2)}, u32[]{:S(2)}) collective-permute-start(bf16[256,1024]{1,0:T(8,128)(2,1)} %refs_0_.1), channel_id=1, source_target_pairs={{1,0},{0,1},{3,2},{2,3},{5,4},{4,5},{7,6},{6,7},{9,8},{8,9},{11,10... | collective-permute-start | bytes 1572872 | tf_op jit(solution)/shard_map/ppermute | solution.py:112
  2.9 28.2 %collective-permute-start.8 = (bf16[256,1024]{1,0:T(8,128)(2,1)}, bf16[256,1024]{1,0:T(8,128)(2,1)S(1)}, u32[]{:S(2)}, u32[]{:S(2)}) collective-permute-start(bf16[256,1024]{1,0:T(8,128)(2,1)} %refs_0_.1), channel_id=1, source_target_pairs={{0,4},{4,8},{8,12},{12,0},{1,5},{5,9},{9,13},{13,1},{2,6},{6,10},{... | collective-permute-start | bytes 1572872 | tf_op jit(solution)/shard_map/ppermute | solution.py:120
  4.5 27.7 %collective-permute-start.6 = (bf16[256,1024]{1,0:T(8,128)(2,1)}, bf16[256,1024]{1,0:T(8,128)(2,1)S(1)}, u32[]{:S(2)}, u32[]{:S(2)}) collective-permute-start(bf16[256,1024]{1,0:T(8,128)(2,1)} %refs_0_.1), channel_id=1, source_target_pairs={{0,8},{12,4},{1,9},{13,5},{2,10},{14,6},{3,11},{15,7},{16,24},{28,... | collective-permute-start | bytes 1572872 | tf_op jit(solution)/shard_map/ppermute | solution.py:120
  15.1 13.7 %collective-permute-start.2 = (bf16[256,1024]{1,0:T(8,128)(2,1)S(1)}, bf16[256,1024]{1,0:T(8,128)(2,1)S(1)}, u32[]{:S(2)}, u32[]{:S(2)}) collective-permute-start(bf16[256,1024]{1,0:T(8,128)(2,1)S(1)} %collective-permute-done.1.refs_2_), channel_id=1, source_target_pairs={{1,0},{0,1},{3,2},{2,3},{5,4},{4,5},{7,6},{6,7},{9,8},{8,9},{11,10... | collective-permute-start | bytes 1572872 | tf_op jit(solution)/shard_map/ppermute | solution.py:112
  16.5 3.6 %collective-permute-start.4 = (s32[2,256]{1,0:T(2,128)S(1)}, s32[2,256]{1,0:T(2,128)S(1)}, u32[]{:S(2)}, u32[]{:S(2)}) collective-permute-start(s32[2,256]{1,0:T(2,128)S(1)} %pad_add_fusion.refs_4_.refs_3_), channel_id=1, source_target_pairs={{2,0},{0,2},{3,1},{1,3},{6,4},{4,6},{7,5},{5,7},{10,8},{8,10},{11,... | collective-permute-start | bytes 6152 | tf_op jit(solution)/shard_map/ppermute | solution.py:112
  20.1 1.2 %collective-permute-start.3 = (s32[2,256]{1,0:T(2,128)S(1)}, s32[2,256]{1,0:T(2,128)S(1)}, u32[]{:S(2)}, u32[]{:S(2)}) collective-permute-start(s32[2,256]{1,0:T(2,128)S(1)} %pad_add_fusion.refs_4_.refs_3_), channel_id=1, source_target_pairs={{1,0},{0,1},{3,2},{2,3},{5,4},{4,5},{7,6},{6,7},{9,8},{8,9},{11,10... | collective-permute-start | bytes 6152 | tf_op jit(solution)/shard_map/ppermute | solution.py:112
  21.3 1.2 %collective-permute-start.5 = (s32[2,256]{1,0:T(2,128)S(1)}, s32[2,256]{1,0:T(2,128)S(1)}, u32[]{:S(2)}, u32[]{:S(2)}) collective-permute-start(s32[2,256]{1,0:T(2,128)S(1)} %collective-permute-done.4.refs_6_.refs_5_), channel_id=1, source_target_pairs={{1,0},{0,1},{3,2},{2,3},{5,4},{4,5},{7,6},{6,7},{9,8},{8,9},{11,10... | collective-permute-start | bytes 6152 | tf_op jit(solution)/shard_map/ppermute | solution.py:112
  22.4 8.7 %collective-permute-start.9 = (s32[2,256]{1,0:T(2,128)S(1)}, s32[2,256]{1,0:T(2,128)S(1)}, u32[]{:S(2)}, u32[]{:S(2)}) collective-permute-start(s32[2,256]{1,0:T(2,128)S(1)} %pad_add_fusion.refs_4_.refs_3_), channel_id=1, source_target_pairs={{0,4},{4,8},{8,12},{12,0},{1,5},{5,9},{9,13},{13,1},{2,6},{6,10},{... | collective-permute-start | bytes 6152 | tf_op jit(solution)/shard_map/ppermute | solution.py:132
  24.2 8.0 %collective-permute-start.7 = (s32[2,256]{1,0:T(2,128)S(1)}, s32[2,256]{1,0:T(2,128)S(1)}, u32[]{:S(2)}, u32[]{:S(2)}) collective-permute-start(s32[2,256]{1,0:T(2,128)S(1)} %pad_add_fusion.refs_4_.refs_3_), channel_id=1, source_target_pairs={{0,8},{12,4},{1,9},{13,5},{2,10},{14,6},{3,11},{15,7},{16,24},{28,... | collective-permute-start | bytes 6152 | tf_op jit(solution)/shard_map/ppermute | solution.py:132
  28.7 1.0 %copy-start = (bf16[256,1024]{1,0:T(8,128)(2,1)S(1)}, bf16[256,1024]{1,0:T(8,128)(2,1)}, u32[]{:S(2)}) copy-start(bf16[256,1024]{1,0:T(8,128)(2,1)} %refs_0_.1) | copy-start | bytes 1572868
  33.3 2.5 %collective-permute-start.10 = (f32[2,256]{1,0:T(2,128)S(1)}, f32[2,256]{1,0:T(2,128)S(1)}, u32[]{:S(2)}, u32[]{:S(2)}) collective-permute-start(f32[2,256]{1,0:T(2,128)S(1)} %get-tuple-element.18), channel_id=1, source_target_pairs={{1,0},{0,1},{3,2},{2,3},{5,4},{4,5},{7,6},{6,7},{9,8},{8,9},{11,10... | collective-permute-start | bytes 6152 | tf_op jit(solution)/shard_map/ppermute | solution.py:112
  33.4 4.5 %collective-permute-start.13 = (f32[1,256]{1,0:T(1,128)S(1)}, f32[1,256]{1,0:T(1,128)S(1)}, u32[]{:S(2)}, u32[]{:S(2)}) collective-permute-start(f32[1,256]{1,0:T(1,128)S(1)} %get-tuple-element.20), channel_id=1, source_target_pairs={{0,8},{4,12},{8,0},{12,4},{1,9},{5,13},{9,1},{13,5},{2,10},{6,14},... | collective-permute-start | bytes 3080 | tf_op jit(solution)/shard_map/ppermute | solution.py:154
  34.4 3.6 %collective-permute-start.12 = (f32[1,256]{1,0:T(1,128)S(1)}, f32[1,256]{1,0:T(1,128)S(1)}, u32[]{:S(2)}, u32[]{:S(2)}) collective-permute-start(f32[1,256]{1,0:T(1,128)S(1)} %get-tuple-element.19), channel_id=1, source_target_pairs={{4,0},{8,4},{12,8},{0,12},{5,1},{9,5},{13,9},{1,13},{6,2},{10,6},{... | collective-permute-start | bytes 3080 | tf_op jit(solution)/shard_map/ppermute | solution.py:154
  35.8 3.6 %collective-permute-start.11 = (f32[1,256]{1,0:T(1,128)S(1)}, f32[1,256]{1,0:T(1,128)S(1)}, u32[]{:S(2)}, u32[]{:S(2)}) collective-permute-start(f32[1,256]{1,0:T(1,128)S(1)} %slice.9), channel_id=1, source_target_pairs={{2,0},{0,2},{3,1},{1,3},{6,4},{4,6},{7,5},{5,7},{10,8},{8,10},{11,... | collective-permute-start | bytes 3080 | tf_op jit(solution)/shard_map/ppermute | solution.py:112

commit v2 on v1

v2 whole, which is shorter than its diff:
```python
import jax
import jax.numpy as jnp
from jax import lax
from jax.experimental import pallas as pl
from jax.experimental.pallas import tpu as pltpu
from jax.sharding import PartitionSpec as P

VMEM_BYTES = 40 * 1024 * 1024
META_ROWS = 8
DIGITS = 4


def prepare_kernel(place, row_total, raw_ref, label_ref, priority_ref, out_ref):
    rows, width = raw_ref.shape
    wide = raw_ref[...].astype(jnp.float32)
    scale = lax.rsqrt(jnp.sum(wide * wide, axis=1, keepdims=True) + 1e-06)
    out_ref[0:rows, :] = (wide * scale).astype(jnp.bfloat16)
    index = lax.broadcasted_iota(jnp.int32, (1, rows), 1)
    key = priority_ref[...] * row_total + place() * rows + index
    digits = jnp.concatenate([(key >> (8 * i)) & 255 for i in range(DIGITS)], axis=1)
    label = jnp.concatenate([label_ref[...] + 1] + [jnp.zeros_like(key)] * (DIGITS - 1), axis=1)
    which = lax.broadcasted_iota(jnp.int32, (META_ROWS, DIGITS * rows), 0)
    extra = jnp.where(which == 0, label, jnp.where(which == 1, digits, 0)).astype(jnp.float32)
    if width > DIGITS * rows:
        zeros = jnp.zeros((META_ROWS, width - DIGITS * rows), jnp.float32)
        extra = jnp.concatenate([extra, zeros], axis=1)
    out_ref[rows : rows + META_ROWS, :] = extra.astype(jnp.bfloat16)


def meta_of(ref, rows):
    extra = ref[rows : rows + META_ROWS, :].astype(jnp.float32).astype(jnp.int32)
    label = extra[0:1, 0:rows]
    key = extra[1:2, 0:rows]
    for i in range(1, DIGITS):
        key = key + (extra[1:2, i * rows : (i + 1) * rows] << (8 * i))
    return label, key


def as_column(row):
    parts = [
        jnp.broadcast_to(row[:, i : i + 128], (128, 128)).T for i in range(0, row.shape[1], 128)
    ]
    return jnp.concatenate(parts, axis=0)


def as_row(column_best):
    parts = [
        jnp.max(column_best[i : i + 128, :].T, axis=0, keepdims=True)
        for i in range(0, column_best.shape[0], 128)
    ]
    return jnp.concatenate(parts, axis=1)


def score_block(left, right, left_label, left_key, label, key):
    scores = lax.dot_general(
        left, right, (((1,), (1,)), ((), ())), preferred_element_type=jnp.float32
    )
    for_left, for_right = None, []
    for i in range(0, scores.shape[1], 128):
        tile = jnp.where(left_label == label[:, i : i + 128], scores[:, i : i + 128], -1.0)
        mine = jnp.where(key[:, i : i + 128] < left_key, tile, -1.0)
        for_left = mine if for_left is None else jnp.maximum(for_left, mine)
        theirs = jnp.where(left_key < key[:, i : i + 128], tile, -1.0)
        for_right.append(jnp.max(theirs, axis=0, keepdims=True))
    return for_left, jnp.concatenate(for_right, axis=1)


def score_kernel(rows, reps, grid, sum_in, left_in, *refs):
    lefts, rights = len(grid), max(max(met) for met in grid if met) + 1
    right_refs, left_refs, refs = refs[:rights], refs[rights : lefts + rights], refs[lefts + rights :]
    old_sums, refs = refs[: reps * sum_in], refs[reps * sum_in :]
    old_lefts, refs = refs[:left_in], refs[left_in:]
    sums, outs = refs[:reps], refs[reps:]
    for r in range(reps):
        sums[r][...] = old_sums[r][...] if sum_in else jnp.full(sums[r].shape, -1.0, jnp.float32)
    for j, met in enumerate(grid):
        left = left_refs[j][0:rows, :]
        left_label, left_key = (as_column(m) for m in meta_of(left_refs[j], rows))
        best = None
        for i in met:
            label, key = meta_of(right_refs[i], rows)
            here, there = score_block(
                left, right_refs[i][0:rows, :], left_label, left_key, label, key
            )
            best = here if best is None else jnp.maximum(best, here)
            if j > 0:
                where = slice(i // reps, i // reps + 1)
                sums[i % reps][where, :] = jnp.maximum(sums[i % reps][where, :], there)
        row = old_lefts[j][...] if j < left_in else None
        if met:
            row = as_row(best) if row is None else jnp.maximum(row, as_row(best))
        outs[j][...] = row


def kernel_call(kernel, out_shape, operands, flops, **options):
    whole = pl.BlockSpec(memory_space=pltpu.VMEM)
    options.setdefault("in_specs", [whole] * len(operands))
    return pl.pallas_call(
        kernel,
        out_shape=out_shape,
        out_specs=[whole] * len(out_shape),
        compiler_params=pltpu.CompilerParams(vmem_limit_bytes=VMEM_BYTES),
        cost_estimate=pl.CostEstimate(
            flops=flops,
            bytes_accessed=sum(o.size * o.dtype.itemsize for o in operands),
            transcendentals=0,
        ),
        **options,
    )(*operands)


def body(embeddings, labels, priority):
    rows, width = embeddings.shape
    owners, helpers, reps = (lax.axis_size(a) for a in ("cluster", "helper", "rep"))
    row_total = rows * owners * helpers * reps
    count = helpers * reps

    def place():
        return lax.axis_index(("cluster", "helper", "rep"))

    (mine,) = kernel_call(
        lambda *refs: prepare_kernel(place, row_total, *refs),
        [jax.ShapeDtypeStruct((rows + META_ROWS, width), jnp.bfloat16)],
        [embeddings, labels.reshape(1, rows), priority.reshape(1, rows)],
        4 * rows * width,
    )

    def shifted(value, axis, size, shift):
        return lax.ppermute(value, axis, [((i + shift) % size, i) for i in range(size)])

    steps = [[(i, (i + d) % owners) for i in range(owners)] for d in range(1, (owners + 1) // 2)]
    backs = [[(b, a) for a, b in step] for step in steps]
    if owners % 2 == 0:
        half = owners // 2
        steps.append([(i, i + half) if i % 2 == 0 else (i + half, i) for i in range(half)])
        backs.append([(i, (i + half) % owners) for i in range(owners)])
    others = [lax.ppermute(mine, "cluster", step) for step in steps]

    def plane_block(h, r):
        pairs = [
            (((i + h) % helpers) * reps + (j + r) % reps, i * reps + j)
            for i in range(helpers)
            for j in range(reps)
        ]
        return lax.ppermute(mine, ("helper", "rep"), pairs) if h or r else mine

    blocks = [plane_block(h, r) for h in range(helpers) for r in range(reps)]

    row = jax.ShapeDtypeStruct((1, rows), jnp.float32)
    per_rep = [jax.ShapeDtypeStruct((helpers, rows), jnp.float32)] * reps

    def score(lefts, grid, sums, bests, flops=None):
        used = max(max(met) for met in grid if met) + 1
        found = kernel_call(
            lambda *refs: score_kernel(rows, reps, grid, bool(sums), len(bests), *refs),
            per_rep + [row] * len(grid),
            [blocks[i] if any(i in met for met in grid) else mine for i in range(used)] + lefts + sums + bests,
            flops or 2 * sum(map(len, grid)) * rows * rows * width,
        )
        return list(found[:reps]), list(found[reps:])

    every = list(range(count))
    far = [i for i in every if i >= reps and i % reps]
    near = [i for i in every if i not in far]
    firsts = [mine] + others[:-1]
    sums, bests = score(firsts, [near] * len(firsts), [], [])
    sums, bests = score([mine] + others, [far] * len(firsts) + [every], sums, bests)
    own_best, *found = bests
    returned = [lax.ppermute(value, "cluster", back) for value, back in zip(found, backs)]
    total = sums[0]
    for r in range(1, reps):
        total = jnp.maximum(total, shifted(sums[r], "rep", reps, reps - r))
    best = jnp.maximum(own_best, total[0:1])
    for h in range(1, helpers):
        best = jnp.maximum(best, shifted(total[h : h + 1], "helper", helpers, helpers - h))
    for value in returned:
        best = jnp.maximum(best, value)
    return best[0]


def solution(mesh):
    axes = ("groups", "cluster", "helper", "rep")
    in_specs = (P(axes, None), P(axes, None), P(axes))
    return jax.shard_map(body, mesh=mesh, in_specs=in_specs, out_specs=P(axes), check_vma=False)
```

time: 40.2 us -> 39.2 us (0.975)
  waiting for transfers between devices: 12.1 us -> 18.9 us
  starting transfers between devices: 21.3 us -> 15 us
  other arithmetic: 1.95 us -> 0.57 us
  Pallas kernels: 3.48 us -> 2.77 us
  local copies, waits for them, and re-layouts: 1.04 us -> 1.74 us
    ppermute x6 -> x7, waiting for transfers between devices: 0.66 us -> 18.9 us  [the longest x2 15.4 us: body(): others = [lax.ppermute(mine, 'cluster', step) for step in steps]]
    ppermute x8 -> x2, waiting for transfers between devices: 11.4 us -> 0.01 us  [shifted(): lax.ppermute(value, axis, [((i + shift) % size, i) for i in range(size)])]
    ppermute x8 -> x2, starting transfers between devices: 6.55 us -> 2.42 us  [shifted(): lax.ppermute(value, axis, [((i + shift) % size, i) for i in range(size)])]
    ppermute x6 -> x7, starting transfers between devices: 14.8 us -> 12.6 us  [the longest x2 7.59 us: body(): others = [lax.ppermute(mine, 'cluster', step) for step in steps]]
    add x2 -> x0, other arithmetic: 1.36 us -> none  [the longest x1 0.68 us: body(): priority * row_total + place * rows + jnp.arange(rows, dtype=jnp.int32)]
    pallas_call x3, Pallas kernels: 3.48 us -> 2.77 us  [kernel_call(): pl.pallas_call(kernel, out_shape=out_shape, out_specs=[whole] * len(out_s...]
    unnamed x2 -> x6, local copies, waits for them, and re-layouts: 1.04 us -> 1.73 us
  transfers between devices with their start and end apart: 14 -> 9, of which waited for: 7 -> 5; matrix products, arithmetic and copies ran while one was open for 3% -> 0% of each run, Pallas kernels for 6% -> 3%
where the time goes in v2:
time: 39.2 us; the launch traced here: 39 us
  waiting for transfers between devices  18.9 us (48%)
  starting transfers between devices  15 us (38%)
  Pallas kernels  2.77 us (7%)
  local copies, waits for them, and re-layouts  1.74 us (4%)
  other arithmetic  0.57 us (1%)
    ppermute x2, waiting for transfers between devices, body(): others = [lax.ppermute(mine, 'cluster', step) for step in steps]  15.4 us
    ppermute x2, starting transfers between devices, body(): others = [lax.ppermute(mine, 'cluster', step) for step in steps]  7.59 us
    ppermute x2, starting transfers between devices, body(): lax.ppermute(value, 'cluster', back)  3.04 us
    pallas_call x3, Pallas kernels, kernel_call(): pl.pallas_call(kernel, out_shape=out_shape, out_specs=[whole] * len(out_s...  2.77 us
    ppermute x2, starting transfers between devices, shifted(): lax.ppermute(value, axis, [((i + shift) % size, i) for i in range(size)])  2.42 us
    ppermute x2, waiting for transfers between devices, body(): lax.ppermute(value, 'cluster', back)  2.24 us
    ppermute x3, starting transfers between devices, plane_block(): return lax.ppermute(mine, ('helper', 'rep'), pairs) if h or r else mine  1.93 us
    unnamed x6, local copies, waits for them, and re-layouts  1.73 us
  transfers between devices with their start and end apart: 9, of which 5 were waited for; matrix products, arithmetic and copies ran while one was open for 0% of the time, Pallas kernels for 3%

profile of v2, /device:TPU:0, one launch (start us, length us, event | category | flops | bytes accessed | tf_op | source)
XLA Modules:
  0.0 39.0 jit_solution(17254634086915221347)
XLA Ops:
  0.0 0.0 copy-start.2
  0.0 0.0 copy-start.1
  0.0 0.7 %copy-done.2 = s32[256]{0:T(256)S(1)} copy-done((s32[256]{0:T(256)S(1)}, s32[256]{0:T(256)}, u32[]{:S(2)}) %copy-start.2) | copy-done | bytes 1048
  0.7 0.0 copy-done.1
  0.7 0.0 copy-start
  0.7 1.0 %copy-done = bf16[256,1024]{1,0:T(8,128)(2,1)S(1)} copy-done((bf16[256,1024]{1,0:T(8,128)(2,1)S(1)}, bf16[256,1024]{1,0:T(8,128)(2,1)}, u32[]{:S(2)}) %copy-start) | copy-done | bytes 524312
  1.7 0.2 shard_map.37.refs_0_.refs_3_.refs_4_
  1.9 3.1 %collective-permute-start.3 = (bf16[264,1024]{1,0:T(8,128)(2,1)S(1)}, bf16[264,1024]{1,0:T(8,128)(2,1)S(1)}, u32[]{:S(2)}, u32[]{:S(2)}) collective-permute-start(bf16[264,1024]{1,0:T(8,128)(2,1)S(1)} %shard_map.37.refs_0_.refs_3_.refs_4_), channel_id=1, source_target_pairs={{0,4},{4,8},{8,12},{12,0},{1,5},{5,9},{9,13},{13,1},{2,6},{6,10},{... | collective-permute-start | bytes 1622024 | tf_op jit(solution)/shard_map/ppermute | solution.py:137
  5.0 1.5 %collective-permute-start.1 = (bf16[264,1024]{1,0:T(8,128)(2,1)S(1)}, bf16[264,1024]{1,0:T(8,128)(2,1)S(1)}, u32[]{:S(2)}, u32[]{:S(2)}) collective-permute-start(bf16[264,1024]{1,0:T(8,128)(2,1)S(1)} %shard_map.37.refs_0_.refs_3_.refs_4_), channel_id=1, source_target_pairs={{2,0},{3,1},{0,2},{1,3},{6,4},{7,5},{4,6},{5,7},{10,8},{11,9},{8,1... | collective-permute-start | bytes 1622024 | tf_op jit(solution)/shard_map/ppermute | solution.py:145
  6.5 0.0 collective-permute-start
  6.5 4.5 %collective-permute-start.4 = (bf16[264,1024]{1,0:T(8,128)(2,1)S(1)}, bf16[264,1024]{1,0:T(8,128)(2,1)S(1)}, u32[]{:S(2)}, u32[]{:S(2)}) collective-permute-start(bf16[264,1024]{1,0:T(8,128)(2,1)S(1)} %shard_map.37.refs_0_.refs_3_.refs_4_), channel_id=1, source_target_pairs={{0,8},{12,4},{1,9},{13,5},{2,10},{14,6},{3,11},{15,7},{16,24},{28,... | collective-permute-start | bytes 1622024 | tf_op jit(solution)/shard_map/ppermute | solution.py:137
  11.0 0.4 %collective-permute-start.2 = (bf16[264,1024]{1,0:T(8,128)(2,1)S(1)}, bf16[264,1024]{1,0:T(8,128)(2,1)S(1)}, u32[]{:S(2)}, u32[]{:S(2)}) collective-permute-start(bf16[264,1024]{1,0:T(8,128)(2,1)S(1)} %shard_map.37.refs_0_.refs_3_.refs_4_), channel_id=1, source_target_pairs={{3,0},{2,1},{1,2},{0,3},{7,4},{6,5},{5,6},{4,7},{11,8},{10,9},{9,1... | collective-permute-start | bytes 1622024 | tf_op jit(solution)/shard_map/ppermute | solution.py:145
  11.5 8.7 %collective-permute-done.3.refs_4_.refs_5_ = bf16[264,1024]{1,0:T(8,128)(2,1)S(1)} collective-permute-done((bf16[264,1024]{1,0:T(8,128)(2,1)S(1)}, bf16[264,1024]{1,0:T(8,128)(2,1)S(1)}, u32[]{:S(2)}, u32[]{:S(2)}) %collective-permute-start.3) | collective-permute-done | bytes 540704 | tf_op jit(solution)/shard_map/ppermute | solution.py:137
  20.1 0.1 collective-permute-done.1.refs_2_
  20.2 0.0 collective-permute-done.refs_1_
  20.2 1.2 %shard_map.38 = (f32[2,256]{1,0:T(2,128)S(1)}, f32[2,256]{1,0:T(2,128)S(1)}, f32[1,256]{1,0:T(1,128)S(1)}, f32[1,256]{1,0:T(1,128)S(1)}) custom-call(bf16[264,1024]{1,0:T(8,128)(2,1)S(1)} %shard_map.37.refs_0_.refs_3_.refs_4_, bf16[264,1024]{1,0:T(8,128)(2,1)S(1)} %collective-permute-done.refs_1_, bf16[264,1024]{1,0:T(8,128)(2,1)S(1)} %collective-permute-done.1.refs_2_, ...), custom_call_target="tpu_custom_call" | custom-call | flops 805306368 | bytes 2703360 | tf_op jit(solution)/shard_map/pallas_call | solution.py:98
  21.5 6.7 %collective-permute-done.4.refs_6_ = bf16[264,1024]{1,0:T(8,128)(2,1)S(1)} collective-permute-done((bf16[264,1024]{1,0:T(8,128)(2,1)S(1)}, bf16[264,1024]{1,0:T(8,128)(2,1)S(1)}, u32[]{:S(2)}, u32[]{:S(2)}) %collective-permute-start.4) | collective-permute-done | bytes 540704 | tf_op jit(solution)/shard_map/ppermute | solution.py:137
  28.2 1.2 %collective-permute-done.2.refs_3_ = bf16[264,1024]{1,0:T(8,128)(2,1)S(1)} collective-permute-done((bf16[264,1024]{1,0:T(8,128)(2,1)S(1)}, bf16[264,1024]{1,0:T(8,128)(2,1)S(1)}, u32[]{:S(2)}, u32[]{:S(2)}) %collective-permute-start.2) | collective-permute-done | bytes 540704 | tf_op jit(solution)/shard_map/ppermute | solution.py:145
  29.3 1.3 %shard_map.39 = (f32[2,256]{1,0:T(2,128)S(1)}, f32[2,256]{1,0:T(2,128)S(1)}, f32[1,256]{1,0:T(1,128)S(1)}, f32[1,256]{1,0:T(1,128)S(1)}, f32[1,256]{1,0:T(1,128)S(1)}) custom-call(bf16[264,1024]{1,0:T(8,128)(2,1)S(1)} %shard_map.37.refs_0_.refs_3_.refs_4_, bf16[264,1024]{1,0:T(8,128)(2,1)S(1)} %collective-permute-done.refs_1_, ...), custom_call_target="tpu_custom_call" | custom-call | flops 805306368 | bytes 3790848 | tf_op jit(solution)/shard_map/pallas_call | solution.py:98
  30.7 0.9 %collective-permute-start.5 = (f32[2,256]{1,0:T(2,128)S(1)}, f32[2,256]{1,0:T(2,128)S(1)}, u32[]{:S(2)}, u32[]{:S(2)}) collective-permute-start(f32[2,256]{1,0:T(2,128)S(1)} %get-tuple-element.20), channel_id=1, source_target_pairs={{1,0},{0,1},{3,2},{2,3},{5,4},{4,5},{7,6},{6,7},{9,8},{8,9},{11,10... | collective-permute-start | bytes 6152 | tf_op jit(solution)/shard_map/ppermute | solution.py:129
  31.5 2.4 %collective-permute-start.7 = (f32[1,256]{1,0:T(1,128)S(1)}, f32[1,256]{1,0:T(1,128)S(1)}, u32[]{:S(2)}, u32[]{:S(2)}) collective-permute-start(f32[1,256]{1,0:T(1,128)S(1)} %get-tuple-element.21), channel_id=1, source_target_pairs={{4,0},{8,4},{12,8},{0,12},{5,1},{9,5},{13,9},{1,13},{6,2},{10,6},{... | collective-permute-start | bytes 3080 | tf_op jit(solution)/shard_map/ppermute | solution.py:169
  33.9 0.7 %collective-permute-start.8 = (f32[1,256]{1,0:T(1,128)S(1)}, f32[1,256]{1,0:T(1,128)S(1)}, u32[]{:S(2)}, u32[]{:S(2)}) collective-permute-start(f32[1,256]{1,0:T(1,128)S(1)} %get-tuple-element.22), channel_id=1, source_target_pairs={{0,8},{4,12},{8,0},{12,4},{1,9},{5,13},{9,1},{13,5},{2,10},{6,14},... | collective-permute-start | bytes 3080 | tf_op jit(solution)/shard_map/ppermute | solution.py:169
  34.6 0.0 collective-permute-done.5
  34.6 1.6 %collective-permute-start.6 = (f32[1,256]{1,0:T(1,128)S(1)}, f32[1,256]{1,0:T(1,128)S(1)}, u32[]{:S(2)}, u32[]{:S(2)}) collective-permute-start(f32[1,256]{1,0:T(1,128)S(1)} %slice.9), channel_id=1, source_target_pairs={{2,0},{0,2},{3,1},{1,3},{6,4},{4,6},{7,5},{5,7},{10,8},{8,10},{11,... | collective-permute-start | bytes 3080 | tf_op jit(solution)/shard_map/ppermute | solution.py:129
  36.2 0.0 collective-permute-done.7
  36.2 2.2 %collective-permute-done.8 = f32[1,256]{1,0:T(1,128)S(1)} collective-permute-done((f32[1,256]{1,0:T(1,128)S(1)}, f32[1,256]{1,0:T(1,128)S(1)}, u32[]{:S(2)}, u32[]{:S(2)}) %collective-permute-start.8) | collective-permute-done | bytes 1056 | tf_op jit(solution)/shard_map/ppermute | solution.py:169
  38.4 0.0 collective-permute-done.6
  38.4 0.6 %fusion.2 = f32[1,256]{1,0:T(1,128)} fusion(f32[1,256]{1,0:T(1,128)S(1)} %collective-permute-done.8, f32[1,256]{1,0:T(1,128)S(1)} %collective-permute-done.7, f32[1,256]{1,0:T(1,128)S(1)} %collective-permute-done.6, f32[1,256]{1,0:T(1,128)S(1)} %get-tuple-element.18, f32[2,256]{1,0:T(2,128)S(1)} %max.15), kind=kLoop, calls=%fused_computation.3 | loop fusion | flops 1024 | bytes 6144 | tf_op jit(solution)/shard_map/max | solution.py:177
  (2 shorter events, 0.0 us)
Async XLA Ops:
  0.0 0.7 %copy-start.2 = (s32[256]{0:T(256)S(1)}, s32[256]{0:T(256)}, u32[]{:S(2)}) copy-start(s32[256]{0:T(256)} %param.5) | copy-start | bytes 3076
  0.0 0.7 %copy-start.1 = (s32[256,1]{0,1:T(1,128)S(1)}, s32[256,1]{0,1:T(1,128)}, u32[]{:S(2)}) copy-start(s32[256,1]{0,1:T(1,128)} %param.4) | copy-start | bytes 3076
  0.7 1.0 %copy-start = (bf16[256,1024]{1,0:T(8,128)(2,1)S(1)}, bf16[256,1024]{1,0:T(8,128)(2,1)}, u32[]{:S(2)}) copy-start(bf16[256,1024]{1,0:T(8,128)(2,1)} %refs_0_.1) | copy-start | bytes 1572868
  1.9 18.2 %collective-permute-start.3 = (bf16[264,1024]{1,0:T(8,128)(2,1)S(1)}, bf16[264,1024]{1,0:T(8,128)(2,1)S(1)}, u32[]{:S(2)}, u32[]{:S(2)}) collective-permute-start(bf16[264,1024]{1,0:T(8,128)(2,1)S(1)} %shard_map.37.refs_0_.refs_3_.refs_4_), channel_id=1, source_target_pairs={{0,4},{4,8},{8,12},{12,0},{1,5},{5,9},{9,13},{13,1},{2,6},{6,10},{... | collective-permute-start | bytes 1622024 | tf_op jit(solution)/shard_map/ppermute | solution.py:137
  5.0 15.2 %collective-permute-start.1 = (bf16[264,1024]{1,0:T(8,128)(2,1)S(1)}, bf16[264,1024]{1,0:T(8,128)(2,1)S(1)}, u32[]{:S(2)}, u32[]{:S(2)}) collective-permute-start(bf16[264,1024]{1,0:T(8,128)(2,1)S(1)} %shard_map.37.refs_0_.refs_3_.refs_4_), channel_id=1, source_target_pairs={{2,0},{3,1},{0,2},{1,3},{6,4},{7,5},{4,6},{5,7},{10,8},{11,9},{8,1... | collective-permute-start | bytes 1622024 | tf_op jit(solution)/shard_map/ppermute | solution.py:145
  6.5 13.7 %collective-permute-start = (bf16[264,1024]{1,0:T(8,128)(2,1)S(1)}, bf16[264,1024]{1,0:T(8,128)(2,1)S(1)}, u32[]{:S(2)}, u32[]{:S(2)}) collective-permute-start(bf16[264,1024]{1,0:T(8,128)(2,1)S(1)} %shard_map.37.refs_0_.refs_3_.refs_4_), channel_id=1, source_target_pairs={{1,0},{0,1},{3,2},{2,3},{5,4},{4,5},{7,6},{6,7},{9,8},{8,9},{11,10... | collective-permute-start | bytes 1622024 | tf_op jit(solution)/shard_map/ppermute | solution.py:145
  6.5 21.7 %collective-permute-start.4 = (bf16[264,1024]{1,0:T(8,128)(2,1)S(1)}, bf16[264,1024]{1,0:T(8,128)(2,1)S(1)}, u32[]{:S(2)}, u32[]{:S(2)}) collective-permute-start(bf16[264,1024]{1,0:T(8,128)(2,1)S(1)} %shard_map.37.refs_0_.refs_3_.refs_4_), channel_id=1, source_target_pairs={{0,8},{12,4},{1,9},{13,5},{2,10},{14,6},{3,11},{15,7},{16,24},{28,... | collective-permute-start | bytes 1622024 | tf_op jit(solution)/shard_map/ppermute | solution.py:137
  11.0 18.3 %collective-permute-start.2 = (bf16[264,1024]{1,0:T(8,128)(2,1)S(1)}, bf16[264,1024]{1,0:T(8,128)(2,1)S(1)}, u32[]{:S(2)}, u32[]{:S(2)}) collective-permute-start(bf16[264,1024]{1,0:T(8,128)(2,1)S(1)} %shard_map.37.refs_0_.refs_3_.refs_4_), channel_id=1, source_target_pairs={{3,0},{2,1},{1,2},{0,3},{7,4},{6,5},{5,6},{4,7},{11,8},{10,9},{9,1... | collective-permute-start | bytes 1622024 | tf_op jit(solution)/shard_map/ppermute | solution.py:145
  30.7 3.9 %collective-permute-start.5 = (f32[2,256]{1,0:T(2,128)S(1)}, f32[2,256]{1,0:T(2,128)S(1)}, u32[]{:S(2)}, u32[]{:S(2)}) collective-permute-start(f32[2,256]{1,0:T(2,128)S(1)} %get-tuple-element.20), channel_id=1, source_target_pairs={{1,0},{0,1},{3,2},{2,3},{5,4},{4,5},{7,6},{6,7},{9,8},{8,9},{11,10... | collective-permute-start | bytes 6152 | tf_op jit(solution)/shard_map/ppermute | solution.py:129
  31.5 4.6 %collective-permute-start.7 = (f32[1,256]{1,0:T(1,128)S(1)}, f32[1,256]{1,0:T(1,128)S(1)}, u32[]{:S(2)}, u32[]{:S(2)}) collective-permute-start(f32[1,256]{1,0:T(1,128)S(1)} %get-tuple-element.21), channel_id=1, source_target_pairs={{4,0},{8,4},{12,8},{0,12},{5,1},{9,5},{13,9},{1,13},{6,2},{10,6},{... | collective-permute-start | bytes 3080 | tf_op jit(solution)/shard_map/ppermute | solution.py:169
  33.9 4.5 %collective-permute-start.8 = (f32[1,256]{1,0:T(1,128)S(1)}, f32[1,256]{1,0:T(1,128)S(1)}, u32[]{:S(2)}, u32[]{:S(2)}) collective-permute-start(f32[1,256]{1,0:T(1,128)S(1)} %get-tuple-element.22), channel_id=1, source_target_pairs={{0,8},{4,12},{8,0},{12,4},{1,9},{5,13},{9,1},{13,5},{2,10},{6,14},... | collective-permute-start | bytes 3080 | tf_op jit(solution)/shard_map/ppermute | solution.py:169
  34.6 3.8 %collective-permute-start.6 = (f32[1,256]{1,0:T(1,128)S(1)}, f32[1,256]{1,0:T(1,128)S(1)}, u32[]{:S(2)}, u32[]{:S(2)}) collective-permute-start(f32[1,256]{1,0:T(1,128)S(1)} %slice.9), channel_id=1, source_target_pairs={{2,0},{0,2},{3,1},{1,3},{6,4},{4,6},{7,5},{5,7},{10,8},{8,10},{11,... | collective-permute-start | bytes 3080 | tf_op jit(solution)/shard_map/ppermute | solution.py:129

commit v3 on v2

--- a/solution.py
+++ b/solution.py
@@ -60,18 +60,18 @@
         tile = jnp.where(left_label == label[:, i : i + 128], scores[:, i : i + 128], -1.0)
         mine = jnp.where(key[:, i : i + 128] < left_key, tile, -1.0)
         for_left = mine if for_left is None else jnp.maximum(for_left, mine)
-        theirs = jnp.where(left_key < key[:, i : i + 128], tile, -1.0)
+        theirs = jnp.where(key[:, i : i + 128] < left_key, -1.0, tile)
         for_right.append(jnp.max(theirs, axis=0, keepdims=True))
     return for_left, jnp.concatenate(for_right, axis=1)
 
 
-def score_kernel(rows, reps, grid, sum_in, left_in, *refs):
+def score_kernel(rows, helpers, reps, grid, sum_in, left_in, sum_out, *refs):
     lefts, rights = len(grid), max(max(met) for met in grid if met) + 1
-    right_refs, left_refs, refs = refs[:rights], refs[rights : lefts + rights], refs[lefts + rights :]
+    left_refs, right_refs, refs = refs[:lefts], refs[lefts : lefts + rights], refs[lefts + rights :]
     old_sums, refs = refs[: reps * sum_in], refs[reps * sum_in :]
     old_lefts, refs = refs[:left_in], refs[left_in:]
-    sums, outs = refs[:reps], refs[reps:]
-    for r in range(reps):
+    sums, outs = refs[: reps * sum_out], refs[reps * sum_out :]
+    for r in range(len(sums)):
         sums[r][...] = old_sums[r][...] if sum_in else jnp.full(sums[r].shape, -1.0, jnp.float32)
     for j, met in enumerate(grid):
         left = left_refs[j][0:rows, :]
@@ -83,9 +83,9 @@
                 left, right_refs[i][0:rows, :], left_label, left_key, label, key
             )
             best = here if best is None else jnp.maximum(best, here)
-            if j > 0:
-                where = slice(i // reps, i // reps + 1)
-                sums[i % reps][where, :] = jnp.maximum(sums[i % reps][where, :], there)
+            if sum_out:
+                rep, where = i // helpers, slice(i % helpers, i % helpers + 1)
+                sums[rep][where, :] = jnp.maximum(sums[rep][where, :], there)
         row = old_lefts[j][...] if j < left_in else None
         if met:
             row = as_row(best) if row is None else jnp.maximum(row, as_row(best))
@@ -133,7 +133,9 @@
     if owners % 2 == 0:
         half = owners // 2
         steps.append([(i, i + half) if i % 2 == 0 else (i + half, i) for i in range(half)])
-        backs.append([(i, (i + half) % owners) for i in range(owners)])
+        back = [(b, a) for a, b in steps[-1]]
+        idle = sorted({i for i, _ in steps[-1]}), sorted({i for _, i in steps[-1]})
+        backs.append(back + list(zip(*idle)))
     others = [lax.ppermute(mine, "cluster", step) for step in steps]
 
     def plane_block(h, r):
@@ -144,29 +146,31 @@
         ]
         return lax.ppermute(mine, ("helper", "rep"), pairs) if h or r else mine
 
-    blocks = [plane_block(h, r) for h in range(helpers) for r in range(reps)]
+    blocks = [plane_block(h, r) for r in range(reps) for h in range(helpers)]
 
     row = jax.ShapeDtypeStruct((1, rows), jnp.float32)
     per_rep = [jax.ShapeDtypeStruct((helpers, rows), jnp.float32)] * reps
 
-    def score(lefts, grid, sums, bests, flops=None):
+    def score(lefts, grid, sums, bests, sum_out=True):
         used = max(max(met) for met in grid if met) + 1
+        rights = [blocks[i] if any(i in met for met in grid) else mine for i in range(used)]
         found = kernel_call(
-            lambda *refs: score_kernel(rows, reps, grid, bool(sums), len(bests), *refs),
-            per_rep + [row] * len(grid),
-            [blocks[i] if any(i in met for met in grid) else mine for i in range(used)] + lefts + sums + bests,
-            flops or 2 * sum(map(len, grid)) * rows * rows * width,
+            lambda *refs: score_kernel(rows, helpers, reps, grid, bool(sums), len(bests), sum_out, *refs),
+            per_rep * sum_out + [row] * len(grid),
+            lefts + rights + sums + bests,
+            2 * sum(map(len, grid)) * rows * rows * width,
         )
-        return list(found[:reps]), list(found[reps:])
+        return list(found[: reps * sum_out]), list(found[reps * sum_out :])
 
     every = list(range(count))
-    far = [i for i in every if i >= reps and i % reps]
+    far = [i for i in every if i >= helpers and i % helpers]
     near = [i for i in every if i not in far]
-    firsts = [mine] + others[:-1]
-    sums, bests = score(firsts, [near] * len(firsts), [], [])
-    sums, bests = score([mine] + others, [far] * len(firsts) + [every], sums, bests)
-    own_best, *found = bests
-    returned = [lax.ppermute(value, "cluster", back) for value, back in zip(found, backs)]
+    sums, found = [], []
+    if others[1:]:
+        sums, found = score(others[:-1], [near] * (len(others) - 1), [], [])
+    sums, found = score(others, [far] * (len(others) - 1) + [every], sums, found)
+    _, (own_best,) = score([mine], [every], [], [], False)
+    returned = [lax.ppermute(v, "cluster", b) for v, b in zip(found[::-1], backs[::-1])]
     total = sums[0]
     for r in range(1, reps):
         total = jnp.maximum(total, shifted(sums[r], "rep", reps, reps - r))

time: 39.2 us -> 38.9 us (level)
  starting transfers between devices: 15 us -> 14.3 us
    ppermute x2, starting transfers between devices: 3.04 us -> 2.39 us  [body(): lax.ppermute(v, 'cluster', b)]
    ppermute x2, waiting for transfers between devices: 15.4 us -> 15.9 us  [body(): others = [lax.ppermute(mine, 'cluster', step) for step in steps]]
    pallas_call x3 -> x4, Pallas kernels: 2.77 us -> 2.93 us  [kernel_call(): pl.pallas_call(kernel, out_shape=out_shape, out_specs=[whole] * len(out_s...]
  transfers between devices with their start and end apart: 9 -> 9, of which waited for: 5 -> 5; matrix products, arithmetic and copies ran while one was open for 0% -> 0% of each run, Pallas kernels for 3% -> 4%
where the time goes in v3:
time: 38.9 us; the launch traced here: 38.8 us
  waiting for transfers between devices  19.1 us (49%)
  starting transfers between devices  14.3 us (37%)
  Pallas kernels  2.93 us (8%)
  local copies, waits for them, and re-layouts  1.74 us (4%)
  other arithmetic  0.57 us (1%)
    ppermute x2, waiting for transfers between devices, body(): others = [lax.ppermute(mine, 'cluster', step) for step in steps]  15.9 us
    ppermute x2, starting transfers between devices, body(): others = [lax.ppermute(mine, 'cluster', step) for step in steps]  7.59 us
    pallas_call x4, Pallas kernels, kernel_call(): pl.pallas_call(kernel, out_shape=out_shape, out_specs=[whole] * len(out_s...  2.93 us
    ppermute x2, starting transfers between devices, shifted(): lax.ppermute(value, axis, [((i + shift) % size, i) for i in range(size)])  2.43 us
    ppermute x2, starting transfers between devices, body(): lax.ppermute(v, 'cluster', b)  2.39 us
    ppermute x2, waiting for transfers between devices, body(): lax.ppermute(v, 'cluster', b)  2 us
    ppermute x3, starting transfers between devices, plane_block(): return lax.ppermute(mine, ('helper', 'rep'), pairs) if h or r else mine  1.93 us
    unnamed x6, local copies, waits for them, and re-layouts  1.73 us
  transfers between devices with their start and end apart: 9, of which 5 were waited for; matrix products, arithmetic and copies ran while one was open for 0% of the time, Pallas kernels for 4%

profile of v3, /device:TPU:0, one launch (start us, length us, event | category | flops | bytes accessed | tf_op | source)
XLA Modules:
  0.0 38.8 jit_solution(10981294378921320441)
XLA Ops:
  0.0 0.0 copy-start.2
  0.0 0.0 copy-start.1
  0.0 0.7 %copy-done.2 = s32[256]{0:T(256)S(1)} copy-done((s32[256]{0:T(256)S(1)}, s32[256]{0:T(256)}, u32[]{:S(2)}) %copy-start.2) | copy-done | bytes 1048
  0.7 0.0 copy-done.1
  0.7 0.0 copy-start
  0.7 1.0 %copy-done = bf16[256,1024]{1,0:T(8,128)(2,1)S(1)} copy-done((bf16[256,1024]{1,0:T(8,128)(2,1)S(1)}, bf16[256,1024]{1,0:T(8,128)(2,1)}, u32[]{:S(2)}) %copy-start) | copy-done | bytes 524312
  1.7 0.2 shard_map.37.refs_0_.refs_1_.refs_2_
  1.9 3.1 %collective-permute-start.3 = (bf16[264,1024]{1,0:T(8,128)(2,1)S(1)}, bf16[264,1024]{1,0:T(8,128)(2,1)S(1)}, u32[]{:S(2)}, u32[]{:S(2)}) collective-permute-start(bf16[264,1024]{1,0:T(8,128)(2,1)S(1)} %shard_map.37.refs_0_.refs_1_.refs_2_), channel_id=1, source_target_pairs={{0,4},{4,8},{8,12},{12,0},{1,5},{5,9},{9,13},{13,1},{2,6},{6,10},{... | collective-permute-start | bytes 1622024 | tf_op jit(solution)/shard_map/ppermute | solution.py:139
  5.0 1.5 %collective-permute-start = (bf16[264,1024]{1,0:T(8,128)(2,1)S(1)}, bf16[264,1024]{1,0:T(8,128)(2,1)S(1)}, u32[]{:S(2)}, u32[]{:S(2)}) collective-permute-start(bf16[264,1024]{1,0:T(8,128)(2,1)S(1)} %shard_map.37.refs_0_.refs_1_.refs_2_), channel_id=1, source_target_pairs={{2,0},{3,1},{0,2},{1,3},{6,4},{7,5},{4,6},{5,7},{10,8},{11,9},{8,1... | collective-permute-start | bytes 1622024 | tf_op jit(solution)/shard_map/ppermute | solution.py:147
  6.5 0.0 collective-permute-start.1
  6.5 4.5 %collective-permute-start.4 = (bf16[264,1024]{1,0:T(8,128)(2,1)S(1)}, bf16[264,1024]{1,0:T(8,128)(2,1)S(1)}, u32[]{:S(2)}, u32[]{:S(2)}) collective-permute-start(bf16[264,1024]{1,0:T(8,128)(2,1)S(1)} %shard_map.37.refs_0_.refs_1_.refs_2_), channel_id=1, source_target_pairs={{0,8},{12,4},{1,9},{13,5},{2,10},{14,6},{3,11},{15,7},{16,24},{28,... | collective-permute-start | bytes 1622024 | tf_op jit(solution)/shard_map/ppermute | solution.py:139
  11.0 0.4 %collective-permute-start.2 = (bf16[264,1024]{1,0:T(8,128)(2,1)S(1)}, bf16[264,1024]{1,0:T(8,128)(2,1)S(1)}, u32[]{:S(2)}, u32[]{:S(2)}) collective-permute-start(bf16[264,1024]{1,0:T(8,128)(2,1)S(1)} %shard_map.37.refs_0_.refs_1_.refs_2_), channel_id=1, source_target_pairs={{3,0},{2,1},{1,2},{0,3},{7,4},{6,5},{5,6},{4,7},{11,8},{10,9},{9,1... | collective-permute-start | bytes 1622024 | tf_op jit(solution)/shard_map/ppermute | solution.py:147
  11.5 8.7 %collective-permute-done.3.refs_0_ = bf16[264,1024]{1,0:T(8,128)(2,1)S(1)} collective-permute-done((bf16[264,1024]{1,0:T(8,128)(2,1)S(1)}, bf16[264,1024]{1,0:T(8,128)(2,1)S(1)}, u32[]{:S(2)}, u32[]{:S(2)}) %collective-permute-start.3) | collective-permute-done | bytes 540704 | tf_op jit(solution)/shard_map/ppermute | solution.py:139
  20.1 0.1 collective-permute-done.refs_2_.refs_3_
  20.2 0.0 collective-permute-done.1.refs_3_.refs_4_
  20.2 0.7 %shard_map.39 = (f32[2,256]{1,0:T(2,128)S(1)}, f32[2,256]{1,0:T(2,128)S(1)}, f32[1,256]{1,0:T(1,128)S(1)}) custom-call(bf16[264,1024]{1,0:T(8,128)(2,1)S(1)} %collective-permute-done.3.refs_0_, bf16[264,1024]{1,0:T(8,128)(2,1)S(1)} %shard_map.37.refs_0_.refs_1_.refs_2_, bf16[264,1024]{1,0:T(8,128)(2,1)S(1)} %collective-permute-done.refs_2_.refs_3_, ...), custom_call_target="tpu_custom_call" | custom-call | flops 402653184 | bytes 2162688 | tf_op jit(solution)/shard_map/pallas_call | solution.py:98
  21.0 7.2 %collective-permute-done.4.refs_1_ = bf16[264,1024]{1,0:T(8,128)(2,1)S(1)} collective-permute-done((bf16[264,1024]{1,0:T(8,128)(2,1)S(1)}, bf16[264,1024]{1,0:T(8,128)(2,1)S(1)}, u32[]{:S(2)}, u32[]{:S(2)}) %collective-permute-start.4) | collective-permute-done | bytes 540704 | tf_op jit(solution)/shard_map/ppermute | solution.py:139
  28.2 1.2 %collective-permute-done.2.refs_4_.refs_5_ = bf16[264,1024]{1,0:T(8,128)(2,1)S(1)} collective-permute-done((bf16[264,1024]{1,0:T(8,128)(2,1)S(1)}, bf16[264,1024]{1,0:T(8,128)(2,1)S(1)}, u32[]{:S(2)}, u32[]{:S(2)}) %collective-permute-start.2) | collective-permute-done | bytes 540704 | tf_op jit(solution)/shard_map/ppermute | solution.py:147
  29.3 1.1 %shard_map.40 = (f32[2,256]{1,0:T(2,128)S(1)}, f32[2,256]{1,0:T(2,128)S(1)}, f32[1,256]{1,0:T(1,128)S(1)}, f32[1,256]{1,0:T(1,128)S(1)}) custom-call(bf16[264,1024]{1,0:T(8,128)(2,1)S(1)} %collective-permute-done.3.refs_0_, bf16[264,1024]{1,0:T(8,128)(2,1)S(1)} %collective-permute-done.4.refs_1_, bf16[264,1024]{1,0:T(8,128)(2,1)S(1)} %shard_map.37.refs_0_.refs_1_.refs_2_, ...), custom_call_target="tpu_custom_call" | custom-call | flops 671088640 | bytes 3249152 | tf_op jit(solution)/shard_map/pallas_call | solution.py:98
  30.5 0.9 %collective-permute-start.5 = (f32[2,256]{1,0:T(2,128)S(1)}, f32[2,256]{1,0:T(2,128)S(1)}, u32[]{:S(2)}, u32[]{:S(2)}) collective-permute-start(f32[2,256]{1,0:T(2,128)S(1)} %get-tuple-element.16), channel_id=1, source_target_pairs={{1,0},{0,1},{3,2},{2,3},{5,4},{4,5},{7,6},{6,7},{9,8},{8,9},{11,10... | collective-permute-start | bytes 6152 | tf_op jit(solution)/shard_map/ppermute | solution.py:129
  31.3 2.4 %collective-permute-start.8 = (f32[1,256]{1,0:T(1,128)S(1)}, f32[1,256]{1,0:T(1,128)S(1)}, u32[]{:S(2)}, u32[]{:S(2)}) collective-permute-start(f32[1,256]{1,0:T(1,128)S(1)} %get-tuple-element.18), channel_id=1, source_target_pairs={{4,0},{8,4},{12,8},{0,12},{5,1},{9,5},{13,9},{1,13},{6,2},{10,6},{... | collective-permute-start | bytes 3080 | tf_op jit(solution)/shard_map/ppermute | solution.py:173
  33.7 0.0 collective-permute-start.7
  33.7 0.0 collective-permute-done.5
  33.7 1.6 %collective-permute-start.6 = (f32[1,256]{1,0:T(1,128)S(1)}, f32[1,256]{1,0:T(1,128)S(1)}, u32[]{:S(2)}, u32[]{:S(2)}) collective-permute-start(f32[1,256]{1,0:T(1,128)S(1)} %slice.9), channel_id=1, source_target_pairs={{2,0},{0,2},{3,1},{1,3},{6,4},{4,6},{7,5},{5,7},{10,8},{8,10},{11,... | collective-permute-start | bytes 3080 | tf_op jit(solution)/shard_map/ppermute | solution.py:129
  35.3 0.9 %shard_map.38 = f32[1,256]{1,0:T(1,128)S(1)} custom-call(bf16[264,1024]{1,0:T(8,128)(2,1)S(1)} %shard_map.37.refs_0_.refs_1_.refs_2_, bf16[264,1024]{1,0:T(8,128)(2,1)S(1)} %shard_map.37.refs_0_.refs_1_.refs_2_, bf16[264,1024]{1,0:T(8,128)(2,1)S(1)} %collective-permute-done.refs_2_.refs_3_, bf16[264,1024]{1,0:T(8,128)(2,1)S(1)} %collective-permute-done.1.refs_3_.refs_4_, ...), custom_call_target="tpu_custom_call" | custom-call | flops 536870912 | bytes 2703360 | tf_op jit(solution)/shard_map/pallas_call | solution.py:98
  36.2 0.0 collective-permute-done.8
  36.2 2.0 %collective-permute-done.7 = f32[1,256]{1,0:T(1,128)S(1)} collective-permute-done((f32[1,256]{1,0:T(1,128)S(1)}, f32[1,256]{1,0:T(1,128)S(1)}, u32[]{:S(2)}, u32[]{:S(2)}) %collective-permute-start.7) | collective-permute-done | bytes 1056 | tf_op jit(solution)/shard_map/ppermute | solution.py:173
  38.2 0.0 collective-permute-done.6
  38.2 0.6 %fusion.2 = f32[1,256]{1,0:T(1,128)} fusion(f32[1,256]{1,0:T(1,128)S(1)} %collective-permute-done.8, f32[1,256]{1,0:T(1,128)S(1)} %collective-permute-done.7, f32[1,256]{1,0:T(1,128)S(1)} %collective-permute-done.6, f32[1,256]{1,0:T(1,128)S(1)} %shard_map.38, f32[2,256]{1,0:T(2,128)S(1)} %max.15), kind=kLoop, calls=%fused_computation.3 | loop fusion | flops 1024 | bytes 6144 | tf_op jit(solution)/shard_map/max | solution.py:181
  (2 shorter events, 0.0 us)
Async XLA Ops:
  0.0 0.7 %copy-start.2 = (s32[256]{0:T(256)S(1)}, s32[256]{0:T(256)}, u32[]{:S(2)}) copy-start(s32[256]{0:T(256)} %param.5) | copy-start | bytes 3076
  0.0 0.7 %copy-start.1 = (s32[256,1]{0,1:T(1,128)S(1)}, s32[256,1]{0,1:T(1,128)}, u32[]{:S(2)}) copy-start(s32[256,1]{0,1:T(1,128)} %param.4) | copy-start | bytes 3076
  0.7 1.0 %copy-start = (bf16[256,1024]{1,0:T(8,128)(2,1)S(1)}, bf16[256,1024]{1,0:T(8,128)(2,1)}, u32[]{:S(2)}) copy-start(bf16[256,1024]{1,0:T(8,128)(2,1)} %refs_0_.1) | copy-start | bytes 1572868
  1.9 18.2 %collective-permute-start.3 = (bf16[264,1024]{1,0:T(8,128)(2,1)S(1)}, bf16[264,1024]{1,0:T(8,128)(2,1)S(1)}, u32[]{:S(2)}, u32[]{:S(2)}) collective-permute-start(bf16[264,1024]{1,0:T(8,128)(2,1)S(1)} %shard_map.37.refs_0_.refs_1_.refs_2_), channel_id=1, source_target_pairs={{0,4},{4,8},{8,12},{12,0},{1,5},{5,9},{9,13},{13,1},{2,6},{6,10},{... | collective-permute-start | bytes 1622024 | tf_op jit(solution)/shard_map/ppermute | solution.py:139
  5.0 15.2 %collective-permute-start = (bf16[264,1024]{1,0:T(8,128)(2,1)S(1)}, bf16[264,1024]{1,0:T(8,128)(2,1)S(1)}, u32[]{:S(2)}, u32[]{:S(2)}) collective-permute-start(bf16[264,1024]{1,0:T(8,128)(2,1)S(1)} %shard_map.37.refs_0_.refs_1_.refs_2_), channel_id=1, source_target_pairs={{2,0},{3,1},{0,2},{1,3},{6,4},{7,5},{4,6},{5,7},{10,8},{11,9},{8,1... | collective-permute-start | bytes 1622024 | tf_op jit(solution)/shard_map/ppermute | solution.py:147
  6.5 13.7 %collective-permute-start.1 = (bf16[264,1024]{1,0:T(8,128)(2,1)S(1)}, bf16[264,1024]{1,0:T(8,128)(2,1)S(1)}, u32[]{:S(2)}, u32[]{:S(2)}) collective-permute-start(bf16[264,1024]{1,0:T(8,128)(2,1)S(1)} %shard_map.37.refs_0_.refs_1_.refs_2_), channel_id=1, source_target_pairs={{1,0},{0,1},{3,2},{2,3},{5,4},{4,5},{7,6},{6,7},{9,8},{8,9},{11,10... | collective-permute-start | bytes 1622024 | tf_op jit(solution)/shard_map/ppermute | solution.py:147
  6.5 21.7 %collective-permute-start.4 = (bf16[264,1024]{1,0:T(8,128)(2,1)S(1)}, bf16[264,1024]{1,0:T(8,128)(2,1)S(1)}, u32[]{:S(2)}, u32[]{:S(2)}) collective-permute-start(bf16[264,1024]{1,0:T(8,128)(2,1)S(1)} %shard_map.37.refs_0_.refs_1_.refs_2_), channel_id=1, source_target_pairs={{0,8},{12,4},{1,9},{13,5},{2,10},{14,6},{3,11},{15,7},{16,24},{28,... | collective-permute-start | bytes 1622024 | tf_op jit(solution)/shard_map/ppermute | solution.py:139
  11.0 18.3 %collective-permute-start.2 = (bf16[264,1024]{1,0:T(8,128)(2,1)S(1)}, bf16[264,1024]{1,0:T(8,128)(2,1)S(1)}, u32[]{:S(2)}, u32[]{:S(2)}) collective-permute-start(bf16[264,1024]{1,0:T(8,128)(2,1)S(1)} %shard_map.37.refs_0_.refs_1_.refs_2_), channel_id=1, source_target_pairs={{3,0},{2,1},{1,2},{0,3},{7,4},{6,5},{5,6},{4,7},{11,8},{10,9},{9,1... | collective-permute-start | bytes 1622024 | tf_op jit(solution)/shard_map/ppermute | solution.py:147
  30.5 3.3 %collective-permute-start.5 = (f32[2,256]{1,0:T(2,128)S(1)}, f32[2,256]{1,0:T(2,128)S(1)}, u32[]{:S(2)}, u32[]{:S(2)}) collective-permute-start(f32[2,256]{1,0:T(2,128)S(1)} %get-tuple-element.16), channel_id=1, source_target_pairs={{1,0},{0,1},{3,2},{2,3},{5,4},{4,5},{7,6},{6,7},{9,8},{8,9},{11,10... | collective-permute-start | bytes 6152 | tf_op jit(solution)/shard_map/ppermute | solution.py:129
  31.3 4.8 %collective-permute-start.8 = (f32[1,256]{1,0:T(1,128)S(1)}, f32[1,256]{1,0:T(1,128)S(1)}, u32[]{:S(2)}, u32[]{:S(2)}) collective-permute-start(f32[1,256]{1,0:T(1,128)S(1)} %get-tuple-element.18), channel_id=1, source_target_pairs={{4,0},{8,4},{12,8},{0,12},{5,1},{9,5},{13,9},{1,13},{6,2},{10,6},{... | collective-permute-start | bytes 3080 | tf_op jit(solution)/shard_map/ppermute | solution.py:173
  33.7 4.5 %collective-permute-start.7 = (f32[1,256]{1,0:T(1,128)S(1)}, f32[1,256]{1,0:T(1,128)S(1)}, u32[]{:S(2)}, u32[]{:S(2)}) collective-permute-start(f32[1,256]{1,0:T(1,128)S(1)} %get-tuple-element.17), channel_id=1, source_target_pairs={{8,0},{4,12},{0,4},{12,8},{9,1},{5,13},{1,5},{13,9},{10,2},{6,14},... | collective-permute-start | bytes 3080 | tf_op jit(solution)/shard_map/ppermute | solution.py:173
  33.7 4.4 %collective-permute-start.6 = (f32[1,256]{1,0:T(1,128)S(1)}, f32[1,256]{1,0:T(1,128)S(1)}, u32[]{:S(2)}, u32[]{:S(2)}) collective-permute-start(f32[1,256]{1,0:T(1,128)S(1)} %slice.9), channel_id=1, source_target_pairs={{2,0},{0,2},{3,1},{1,3},{6,4},{4,6},{7,5},{5,7},{10,8},{8,10},{11,... | collective-permute-start | bytes 3080 | tf_op jit(solution)/shard_map/ppermute | solution.py:129

commit v4 on v3

--- a/solution.py
+++ b/solution.py
@@ -65,14 +65,14 @@
     return for_left, jnp.concatenate(for_right, axis=1)
 
 
-def score_kernel(rows, helpers, reps, grid, sum_in, left_in, sum_out, *refs):
+def score_kernel(rows, helpers, grid, sum_in, left_in, sum_out, *refs):
     lefts, rights = len(grid), max(max(met) for met in grid if met) + 1
     left_refs, right_refs, refs = refs[:lefts], refs[lefts : lefts + rights], refs[lefts + rights :]
-    old_sums, refs = refs[: reps * sum_in], refs[reps * sum_in :]
+    old_sums, refs = refs[: helpers * sum_in], refs[helpers * sum_in :]
     old_lefts, refs = refs[:left_in], refs[left_in:]
-    sums, outs = refs[: reps * sum_out], refs[reps * sum_out :]
-    for r in range(len(sums)):
-        sums[r][...] = old_sums[r][...] if sum_in else jnp.full(sums[r].shape, -1.0, jnp.float32)
+    sums, outs = refs[: helpers * sum_out], refs[helpers * sum_out :]
+    for h in range(len(sums)):
+        sums[h][...] = old_sums[h][...] if sum_in else jnp.full(sums[h].shape, -1.0, jnp.float32)
     for j, met in enumerate(grid):
         left = left_refs[j][0:rows, :]
         left_label, left_key = (as_column(m) for m in meta_of(left_refs[j], rows))
@@ -84,8 +84,8 @@
             )
             best = here if best is None else jnp.maximum(best, here)
             if sum_out:
-                rep, where = i // helpers, slice(i % helpers, i % helpers + 1)
-                sums[rep][where, :] = jnp.maximum(sums[rep][where, :], there)
+                h, where = i % helpers, slice(i // helpers, i // helpers + 1)
+                sums[h][where, :] = jnp.maximum(sums[h][where, :], there)
         row = old_lefts[j][...] if j < left_in else None
         if met:
             row = as_row(best) if row is None else jnp.maximum(row, as_row(best))
@@ -149,18 +149,18 @@
     blocks = [plane_block(h, r) for r in range(reps) for h in range(helpers)]
 
     row = jax.ShapeDtypeStruct((1, rows), jnp.float32)
-    per_rep = [jax.ShapeDtypeStruct((helpers, rows), jnp.float32)] * reps
+    per_helper = [jax.ShapeDtypeStruct((reps, rows), jnp.float32)] * helpers
 
     def score(lefts, grid, sums, bests, sum_out=True):
         used = max(max(met) for met in grid if met) + 1
         rights = [blocks[i] if any(i in met for met in grid) else mine for i in range(used)]
         found = kernel_call(
-            lambda *refs: score_kernel(rows, helpers, reps, grid, bool(sums), len(bests), sum_out, *refs),
-            per_rep * sum_out + [row] * len(grid),
+            lambda *refs: score_kernel(rows, helpers, grid, bool(sums), len(bests), sum_out, *refs),
+            per_helper * sum_out + [row] * len(grid),
             lefts + rights + sums + bests,
             2 * sum(map(len, grid)) * rows * rows * width,
         )
-        return list(found[: reps * sum_out]), list(found[reps * sum_out :])
+        return list(found[: helpers * sum_out]), list(found[helpers * sum_out :])
 
     every = list(range(count))
     far = [i for i in every if i >= helpers and i % helpers]
@@ -170,13 +170,13 @@
         sums, found = score(others[:-1], [near] * (len(others) - 1), [], [])
     sums, found = score(others, [far] * (len(others) - 1) + [every], sums, found)
     _, (own_best,) = score([mine], [every], [], [], False)
-    returned = [lax.ppermute(v, "cluster", b) for v, b in zip(found[::-1], backs[::-1])]
+    returned = [lax.ppermute(v, "cluster", b) for v, b in zip(found, backs)]
     total = sums[0]
+    for h in range(1, helpers):
+        total = jnp.maximum(total, shifted(sums[h], "helper", helpers, helpers - h))
+    best = jnp.maximum(own_best, total[0:1])
     for r in range(1, reps):
-        total = jnp.maximum(total, shifted(sums[r], "rep", reps, reps - r))
-    best = jnp.maximum(own_best, total[0:1])
-    for h in range(1, helpers):
-        best = jnp.maximum(best, shifted(total[h : h + 1], "helper", helpers, helpers - h))
+        best = jnp.maximum(best, shifted(total[r : r + 1], "rep", reps, reps - r))
     for value in returned:
         best = jnp.maximum(best, value)
     return best[0]

time: 38.9 us -> 38.6 us (level)
  waiting for transfers between devices: 19.1 us -> 17.5 us
  starting transfers between devices: 14.3 us -> 15.7 us
    ppermute x2, starting transfers between devices: 2.39 us -> 5.01 us  [body(): returned = [lax.ppermute(v, 'cluster', b) for v, b in zip(found, backs)]]
    ppermute x2, waiting for transfers between devices: 2 us -> 0.33 us  [body(): returned = [lax.ppermute(v, 'cluster', b) for v, b in zip(found, backs)]]
    ppermute x2, starting transfers between devices: 2.43 us -> 1.13 us  [shifted(): lax.ppermute(value, axis, [((i + shift) % size, i) for i in range(size)])]
where the time goes in v4:
time: 38.6 us; the launch traced here: 38.4 us
  waiting for transfers between devices  17.5 us (45%)
  starting transfers between devices  15.7 us (41%)
  Pallas kernels  2.93 us (8%)
  local copies, waits for them, and re-layouts  1.74 us (5%)
  other arithmetic  0.57 us (1%)
    ppermute x2, waiting for transfers between devices, body(): others = [lax.ppermute(mine, 'cluster', step) for step in steps]  15.9 us
    ppermute x2, starting transfers between devices, body(): others = [lax.ppermute(mine, 'cluster', step) for step in steps]  7.59 us
    ppermute x2, starting transfers between devices, body(): returned = [lax.ppermute(v, 'cluster', b) for v, b in zip(found, backs)]  5.01 us
    pallas_call x4, Pallas kernels, kernel_call(): pl.pallas_call(kernel, out_shape=out_shape, out_specs=[whole] * len(out_s...  2.93 us
    ppermute x3, starting transfers between devices, plane_block(): return lax.ppermute(mine, ('helper', 'rep'), pairs) if h or r else mine  1.93 us
    unnamed x6, local copies, waits for them, and re-layouts  1.73 us
    ppermute x3, waiting for transfers between devices, plane_block(): return lax.ppermute(mine, ('helper', 'rep'), pairs) if h or r else mine  1.24 us
    ppermute x2, starting transfers between devices, shifted(): lax.ppermute(value, axis, [((i + shift) % size, i) for i in range(size)])  1.13 us
  transfers between devices with their start and end apart: 9, of which 5 were waited for; matrix products, arithmetic and copies ran while one was open for 0% of the time, Pallas kernels for 4%

profile of v4, /device:TPU:0, one launch (start us, length us, event | category | flops | bytes accessed | tf_op | source)
XLA Modules:
  0.0 38.4 jit_solution(2172259266754512302)
XLA Ops:
  0.0 0.0 copy-start.2
  0.0 0.0 copy-start.1
  0.0 0.7 %copy-done.2 = s32[256]{0:T(256)S(1)} copy-done((s32[256]{0:T(256)S(1)}, s32[256]{0:T(256)}, u32[]{:S(2)}) %copy-start.2) | copy-done | bytes 1048
  0.7 0.0 copy-done.1
  0.7 0.0 copy-start
  0.7 1.0 %copy-done = bf16[256,1024]{1,0:T(8,128)(2,1)S(1)} copy-done((bf16[256,1024]{1,0:T(8,128)(2,1)S(1)}, bf16[256,1024]{1,0:T(8,128)(2,1)}, u32[]{:S(2)}) %copy-start) | copy-done | bytes 524312
  1.7 0.2 shard_map.37.refs_0_.refs_1_.refs_2_
  1.9 3.1 %collective-permute-start.3 = (bf16[264,1024]{1,0:T(8,128)(2,1)S(1)}, bf16[264,1024]{1,0:T(8,128)(2,1)S(1)}, u32[]{:S(2)}, u32[]{:S(2)}) collective-permute-start(bf16[264,1024]{1,0:T(8,128)(2,1)S(1)} %shard_map.37.refs_0_.refs_1_.refs_2_), channel_id=1, source_target_pairs={{0,4},{4,8},{8,12},{12,0},{1,5},{5,9},{9,13},{13,1},{2,6},{6,10},{... | collective-permute-start | bytes 1622024 | tf_op jit(solution)/shard_map/ppermute | solution.py:139
  5.0 1.5 %collective-permute-start = (bf16[264,1024]{1,0:T(8,128)(2,1)S(1)}, bf16[264,1024]{1,0:T(8,128)(2,1)S(1)}, u32[]{:S(2)}, u32[]{:S(2)}) collective-permute-start(bf16[264,1024]{1,0:T(8,128)(2,1)S(1)} %shard_map.37.refs_0_.refs_1_.refs_2_), channel_id=1, source_target_pairs={{2,0},{3,1},{0,2},{1,3},{6,4},{7,5},{4,6},{5,7},{10,8},{11,9},{8,1... | collective-permute-start | bytes 1622024 | tf_op jit(solution)/shard_map/ppermute | solution.py:147
  6.5 0.0 collective-permute-start.1
  6.5 4.5 %collective-permute-start.4 = (bf16[264,1024]{1,0:T(8,128)(2,1)S(1)}, bf16[264,1024]{1,0:T(8,128)(2,1)S(1)}, u32[]{:S(2)}, u32[]{:S(2)}) collective-permute-start(bf16[264,1024]{1,0:T(8,128)(2,1)S(1)} %shard_map.37.refs_0_.refs_1_.refs_2_), channel_id=1, source_target_pairs={{0,8},{12,4},{1,9},{13,5},{2,10},{14,6},{3,11},{15,7},{16,24},{28,... | collective-permute-start | bytes 1622024 | tf_op jit(solution)/shard_map/ppermute | solution.py:139
  11.0 0.4 %collective-permute-start.2 = (bf16[264,1024]{1,0:T(8,128)(2,1)S(1)}, bf16[264,1024]{1,0:T(8,128)(2,1)S(1)}, u32[]{:S(2)}, u32[]{:S(2)}) collective-permute-start(bf16[264,1024]{1,0:T(8,128)(2,1)S(1)} %shard_map.37.refs_0_.refs_1_.refs_2_), channel_id=1, source_target_pairs={{3,0},{2,1},{1,2},{0,3},{7,4},{6,5},{5,6},{4,7},{11,8},{10,9},{9,1... | collective-permute-start | bytes 1622024 | tf_op jit(solution)/shard_map/ppermute | solution.py:147
  11.5 8.7 %collective-permute-done.3.refs_0_ = bf16[264,1024]{1,0:T(8,128)(2,1)S(1)} collective-permute-done((bf16[264,1024]{1,0:T(8,128)(2,1)S(1)}, bf16[264,1024]{1,0:T(8,128)(2,1)S(1)}, u32[]{:S(2)}, u32[]{:S(2)}) %collective-permute-start.3) | collective-permute-done | bytes 540704 | tf_op jit(solution)/shard_map/ppermute | solution.py:139
  20.1 0.1 collective-permute-done.refs_2_.refs_3_
  20.2 0.0 collective-permute-done.1.refs_3_.refs_4_
  20.2 0.7 %shard_map.39 = (f32[2,256]{1,0:T(2,128)S(1)}, f32[2,256]{1,0:T(2,128)S(1)}, f32[1,256]{1,0:T(1,128)S(1)}) custom-call(bf16[264,1024]{1,0:T(8,128)(2,1)S(1)} %collective-permute-done.3.refs_0_, bf16[264,1024]{1,0:T(8,128)(2,1)S(1)} %shard_map.37.refs_0_.refs_1_.refs_2_, bf16[264,1024]{1,0:T(8,128)(2,1)S(1)} %collective-permute-done.refs_2_.refs_3_, ...), custom_call_target="tpu_custom_call" | custom-call | flops 402653184 | bytes 2162688 | tf_op jit(solution)/shard_map/pallas_call | solution.py:98
  21.0 7.2 %collective-permute-done.4.refs_1_ = bf16[264,1024]{1,0:T(8,128)(2,1)S(1)} collective-permute-done((bf16[264,1024]{1,0:T(8,128)(2,1)S(1)}, bf16[264,1024]{1,0:T(8,128)(2,1)S(1)}, u32[]{:S(2)}, u32[]{:S(2)}) %collective-permute-start.4) | collective-permute-done | bytes 540704 | tf_op jit(solution)/shard_map/ppermute | solution.py:139
  28.2 1.2 %collective-permute-done.2.refs_4_.refs_5_ = bf16[264,1024]{1,0:T(8,128)(2,1)S(1)} collective-permute-done((bf16[264,1024]{1,0:T(8,128)(2,1)S(1)}, bf16[264,1024]{1,0:T(8,128)(2,1)S(1)}, u32[]{:S(2)}, u32[]{:S(2)}) %collective-permute-start.2) | collective-permute-done | bytes 540704 | tf_op jit(solution)/shard_map/ppermute | solution.py:147
  29.3 1.1 %shard_map.40 = (f32[2,256]{1,0:T(2,128)S(1)}, f32[2,256]{1,0:T(2,128)S(1)}, f32[1,256]{1,0:T(1,128)S(1)}, f32[1,256]{1,0:T(1,128)S(1)}) custom-call(bf16[264,1024]{1,0:T(8,128)(2,1)S(1)} %collective-permute-done.3.refs_0_, bf16[264,1024]{1,0:T(8,128)(2,1)S(1)} %collective-permute-done.4.refs_1_, bf16[264,1024]{1,0:T(8,128)(2,1)S(1)} %shard_map.37.refs_0_.refs_1_.refs_2_, ...), custom_call_target="tpu_custom_call" | custom-call | flops 671088640 | bytes 3249152 | tf_op jit(solution)/shard_map/pallas_call | solution.py:98
  30.5 1.1 %collective-permute-start.5 = (f32[2,256]{1,0:T(2,128)S(1)}, f32[2,256]{1,0:T(2,128)S(1)}, u32[]{:S(2)}, u32[]{:S(2)}) collective-permute-start(f32[2,256]{1,0:T(2,128)S(1)} %get-tuple-element.16), channel_id=1, source_target_pairs={{2,0},{0,2},{3,1},{1,3},{6,4},{4,6},{7,5},{5,7},{10,8},{8,10},{11,... | collective-permute-start | bytes 6152 | tf_op jit(solution)/shard_map/ppermute | solution.py:129
  31.5 2.6 %collective-permute-start.8 = (f32[1,256]{1,0:T(1,128)S(1)}, f32[1,256]{1,0:T(1,128)S(1)}, u32[]{:S(2)}, u32[]{:S(2)}) collective-permute-start(f32[1,256]{1,0:T(1,128)S(1)} %get-tuple-element.18), channel_id=1, source_target_pairs={{8,0},{4,12},{0,4},{12,8},{9,1},{5,13},{1,5},{13,9},{10,2},{6,14},... | collective-permute-start | bytes 3080 | tf_op jit(solution)/shard_map/ppermute | solution.py:173
  34.1 2.4 %collective-permute-start.7 = (f32[1,256]{1,0:T(1,128)S(1)}, f32[1,256]{1,0:T(1,128)S(1)}, u32[]{:S(2)}, u32[]{:S(2)}) collective-permute-start(f32[1,256]{1,0:T(1,128)S(1)} %get-tuple-element.17), channel_id=1, source_target_pairs={{4,0},{8,4},{12,8},{0,12},{5,1},{9,5},{13,9},{1,13},{6,2},{10,6},{... | collective-permute-start | bytes 3080 | tf_op jit(solution)/shard_map/ppermute | solution.py:173
  36.6 0.0 collective-permute-done.5
  36.6 0.1 collective-permute-start.6
  36.6 0.9 %shard_map.38 = f32[1,256]{1,0:T(1,128)S(1)} custom-call(bf16[264,1024]{1,0:T(8,128)(2,1)S(1)} %shard_map.37.refs_0_.refs_1_.refs_2_, bf16[264,1024]{1,0:T(8,128)(2,1)S(1)} %shard_map.37.refs_0_.refs_1_.refs_2_, bf16[264,1024]{1,0:T(8,128)(2,1)S(1)} %collective-permute-done.refs_2_.refs_3_, bf16[264,1024]{1,0:T(8,128)(2,1)S(1)} %collective-permute-done.1.refs_3_.refs_4_, ...), custom_call_target="tpu_custom_call" | custom-call | flops 536870912 | bytes 2703360 | tf_op jit(solution)/shard_map/pallas_call | solution.py:98
  37.5 0.0 collective-permute-done.8
  37.5 0.3 collective-permute-done.7
  37.9 0.0 collective-permute-done.6
  37.9 0.6 %fusion.2 = f32[1,256]{1,0:T(1,128)} fusion(f32[1,256]{1,0:T(1,128)S(1)} %collective-permute-done.8, f32[1,256]{1,0:T(1,128)S(1)} %collective-permute-done.7, f32[1,256]{1,0:T(1,128)S(1)} %collective-permute-done.6, f32[1,256]{1,0:T(1,128)S(1)} %shard_map.38, f32[2,256]{1,0:T(2,128)S(1)} %max.15), kind=kLoop, calls=%fused_computation.3 | loop fusion | flops 1024 | bytes 6144 | tf_op jit(solution)/shard_map/max | solution.py:181
  (2 shorter events, 0.0 us)
Async XLA Ops:
  0.0 0.7 %copy-start.2 = (s32[256]{0:T(256)S(1)}, s32[256]{0:T(256)}, u32[]{:S(2)}) copy-start(s32[256]{0:T(256)} %param.5) | copy-start | bytes 3076
  0.0 0.7 %copy-start.1 = (s32[256,1]{0,1:T(1,128)S(1)}, s32[256,1]{0,1:T(1,128)}, u32[]{:S(2)}) copy-start(s32[256,1]{0,1:T(1,128)} %param.4) | copy-start | bytes 3076
  0.7 1.0 %copy-start = (bf16[256,1024]{1,0:T(8,128)(2,1)S(1)}, bf16[256,1024]{1,0:T(8,128)(2,1)}, u32[]{:S(2)}) copy-start(bf16[256,1024]{1,0:T(8,128)(2,1)} %refs_0_.1) | copy-start | bytes 1572868
  1.9 18.2 %collective-permute-start.3 = (bf16[264,1024]{1,0:T(8,128)(2,1)S(1)}, bf16[264,1024]{1,0:T(8,128)(2,1)S(1)}, u32[]{:S(2)}, u32[]{:S(2)}) collective-permute-start(bf16[264,1024]{1,0:T(8,128)(2,1)S(1)} %shard_map.37.refs_0_.refs_1_.refs_2_), channel_id=1, source_target_pairs={{0,4},{4,8},{8,12},{12,0},{1,5},{5,9},{9,13},{13,1},{2,6},{6,10},{... | collective-permute-start | bytes 1622024 | tf_op jit(solution)/shard_map/ppermute | solution.py:139
  5.0 15.2 %collective-permute-start = (bf16[264,1024]{1,0:T(8,128)(2,1)S(1)}, bf16[264,1024]{1,0:T(8,128)(2,1)S(1)}, u32[]{:S(2)}, u32[]{:S(2)}) collective-permute-start(bf16[264,1024]{1,0:T(8,128)(2,1)S(1)} %shard_map.37.refs_0_.refs_1_.refs_2_), channel_id=1, source_target_pairs={{2,0},{3,1},{0,2},{1,3},{6,4},{7,5},{4,6},{5,7},{10,8},{11,9},{8,1... | collective-permute-start | bytes 1622024 | tf_op jit(solution)/shard_map/ppermute | solution.py:147
  6.5 13.7 %collective-permute-start.1 = (bf16[264,1024]{1,0:T(8,128)(2,1)S(1)}, bf16[264,1024]{1,0:T(8,128)(2,1)S(1)}, u32[]{:S(2)}, u32[]{:S(2)}) collective-permute-start(bf16[264,1024]{1,0:T(8,128)(2,1)S(1)} %shard_map.37.refs_0_.refs_1_.refs_2_), channel_id=1, source_target_pairs={{1,0},{0,1},{3,2},{2,3},{5,4},{4,5},{7,6},{6,7},{9,8},{8,9},{11,10... | collective-permute-start | bytes 1622024 | tf_op jit(solution)/shard_map/ppermute | solution.py:147
  6.5 21.7 %collective-permute-start.4 = (bf16[264,1024]{1,0:T(8,128)(2,1)S(1)}, bf16[264,1024]{1,0:T(8,128)(2,1)S(1)}, u32[]{:S(2)}, u32[]{:S(2)}) collective-permute-start(bf16[264,1024]{1,0:T(8,128)(2,1)S(1)} %shard_map.37.refs_0_.refs_1_.refs_2_), channel_id=1, source_target_pairs={{0,8},{12,4},{1,9},{13,5},{2,10},{14,6},{3,11},{15,7},{16,24},{28,... | collective-permute-start | bytes 1622024 | tf_op jit(solution)/shard_map/ppermute | solution.py:139
  11.0 18.3 %collective-permute-start.2 = (bf16[264,1024]{1,0:T(8,128)(2,1)S(1)}, bf16[264,1024]{1,0:T(8,128)(2,1)S(1)}, u32[]{:S(2)}, u32[]{:S(2)}) collective-permute-start(bf16[264,1024]{1,0:T(8,128)(2,1)S(1)} %shard_map.37.refs_0_.refs_1_.refs_2_), channel_id=1, source_target_pairs={{3,0},{2,1},{1,2},{0,3},{7,4},{6,5},{5,6},{4,7},{11,8},{10,9},{9,1... | collective-permute-start | bytes 1622024 | tf_op jit(solution)/shard_map/ppermute | solution.py:147
  30.5 6.1 %collective-permute-start.5 = (f32[2,256]{1,0:T(2,128)S(1)}, f32[2,256]{1,0:T(2,128)S(1)}, u32[]{:S(2)}, u32[]{:S(2)}) collective-permute-start(f32[2,256]{1,0:T(2,128)S(1)} %get-tuple-element.16), channel_id=1, source_target_pairs={{2,0},{0,2},{3,1},{1,3},{6,4},{4,6},{7,5},{5,7},{10,8},{8,10},{11,... | collective-permute-start | bytes 6152 | tf_op jit(solution)/shard_map/ppermute | solution.py:129
  31.5 6.0 %collective-permute-start.8 = (f32[1,256]{1,0:T(1,128)S(1)}, f32[1,256]{1,0:T(1,128)S(1)}, u32[]{:S(2)}, u32[]{:S(2)}) collective-permute-start(f32[1,256]{1,0:T(1,128)S(1)} %get-tuple-element.18), channel_id=1, source_target_pairs={{8,0},{4,12},{0,4},{12,8},{9,1},{5,13},{1,5},{13,9},{10,2},{6,14},... | collective-permute-start | bytes 3080 | tf_op jit(solution)/shard_map/ppermute | solution.py:173
  34.1 3.7 %collective-permute-start.7 = (f32[1,256]{1,0:T(1,128)S(1)}, f32[1,256]{1,0:T(1,128)S(1)}, u32[]{:S(2)}, u32[]{:S(2)}) collective-permute-start(f32[1,256]{1,0:T(1,128)S(1)} %get-tuple-element.17), channel_id=1, source_target_pairs={{4,0},{8,4},{12,8},{0,12},{5,1},{9,5},{13,9},{1,13},{6,2},{10,6},{... | collective-permute-start | bytes 3080 | tf_op jit(solution)/shard_map/ppermute | solution.py:173
  36.6 1.3 %collective-permute-start.6 = (f32[1,256]{1,0:T(1,128)S(1)}, f32[1,256]{1,0:T(1,128)S(1)}, u32[]{:S(2)}, u32[]{:S(2)}) collective-permute-start(f32[1,256]{1,0:T(1,128)S(1)} %slice.9), channel_id=1, source_target_pairs={{1,0},{0,1},{3,2},{2,3},{5,4},{4,5},{7,6},{6,7},{9,8},{8,9},{11,10... | collective-permute-start | bytes 3080 | tf_op jit(solution)/shard_map/ppermute | solution.py:129
